TPU v7x, 32 devices: a whole 2x2x4 slice. The times are simulated.
32 devices in a mesh: dp: 8 (over z, x), seq: 4 (over y, core).
Axes of the slice: x: 2, y: 2, z: 4, core: 2. Of those that a mesh axis runs over, the one named last changes fastest.
Arguments:
- hidden_in: bfloat16 [16, 2048, 768], P('dp', 'seq'), may hold values from -6 to 6
- cotangent: bfloat16 [16, 2048, 768], P('dp', 'seq'), may hold values from -6 to 6
- lengths: int32 [16], P('dp'), may hold values from 128 to 2048, as said below
- qkv_weight: bfloat16 [768, 2304], P('dp'), may hold values from -0.21875 to 0.21875
- q_bias: bfloat16 [768], P('dp'), may hold values from -3 to 3
- v_bias: bfloat16 [768], P('dp'), may hold values from -0.4375 to 0.4375
- out_weight: bfloat16 [768, 768], P('dp'), may hold values from -6 to 6
- out_bias: bfloat16 [768], P('dp'), may hold values from -3 to 3
- norm1_gain: bfloat16 [768], P('dp'), may hold values from 0.099609375 to 1.8984375
- norm1_shift: bfloat16 [768], P('dp'), may hold values from -3 to 3
- up_weight: bfloat16 [768, 3072], P('dp'), may hold values from -0.21875 to 0.21875
- up_bias: bfloat16 [3072], P('dp'), may hold values from -3 to 3
- down_weight: bfloat16 [3072, 768], P('dp'), may hold values from -0.109375 to 0.109375
- down_bias: bfloat16 [768], P('dp'), may hold values from -3 to 3
- norm2_gain: bfloat16 [768], P('dp'), may hold values from 0.099609375 to 1.8984375
- norm2_shift: bfloat16 [768], P('dp'), may hold values from -3 to 3
Outputs:
- out_hidden: bfloat16 [16, 2048, 768], P('dp', 'seq')
- grad_hidden: bfloat16 [16, 2048, 768], P('dp', 'seq')
- grad_qkv_weight: float32 [768, 2304], P('dp')
- grad_q_bias: float32 [768], P('dp')
- grad_v_bias: float32 [768], P('dp')
- grad_out_weight: float32 [768, 768], P('dp')
- grad_out_bias: float32 [768], P('dp')
- grad_norm1_gain: float32 [768], P('dp')
- grad_norm1_shift: float32 [768], P('dp')
- grad_up_weight: float32 [768, 3072], P('dp')
- grad_up_bias: float32 [3072], P('dp')
- grad_down_weight: float32 [3072, 768], P('dp')
- grad_down_bias: float32 [768], P('dp')
- grad_norm2_gain: float32 [768], P('dp')
- grad_norm2_shift: float32 [768], P('dp')
Inputs may be any that keep to these rules, and one draw needn't show every extreme that they name: `lengths`: of the sequences 0 to 1, 2 to 3 and so on, one in each run has length 2048.
All inputs are finite; a program needn't handle non-finite values.
Results may differ from a plain program's by a relative error of at most 0.017.
The roundings to bfloat16 on the way count: a program that leaves them out, or rounds other values in their place, can miss the bound.
Values may be sent and summed in bfloat16 or wider, within the bound.
A program may use at most 192 MiB of HBM per device.

v0:
```python
import jax
import jax.numpy as jnp
from jax import lax
from jax.sharding import PartitionSpec as P

HD = 64


epsilon = 1e-06


def norm_rows(values_in, gain_vec, shift_vec):
    centered = values_in - jnp.mean(values_in, axis=-1, keepdims=True)
    variance = jnp.mean(centered * centered, axis=-1, keepdims=True)
    return centered * lax.rsqrt(variance + epsilon) * gain_vec + shift_vec


def gelu_exact(values_in):
    return jax.nn.gelu(values_in, approximate=False)


def matmul(first_op, second_op):
    return jnp.dot(first_op, second_op, preferred_element_type=jnp.float32)


def inner_rows(first_op, second_op):
    return lax.dot_general(
        first_op, second_op, (((0,), (0,)), ((), ())), preferred_element_type=jnp.float32
    )


def inner_cols(first_op, second_op):
    return lax.dot_general(
        first_op, second_op, (((1,), (1,)), ((), ())), preferred_element_type=jnp.float32
    )


def masked_scores(query_part, keys_all, key_valid, score_scale):
    scores = (
        jnp.einsum("qhd,khd->hqk", query_part, keys_all, preferred_element_type=jnp.float32)
        * score_scale
    )
    return jnp.where(key_valid, scores, -1e30)


def attend_forward(queries, keys_all, values_all, length, score_scale, block_rows):
    key_count, heads_here, head_size = keys_all.shape
    key_valid = (jnp.arange(key_count) < length)[None, None, :]
    block_count = key_count // block_rows
    query_blocks = queries.reshape(block_count, block_rows, heads_here, head_size)

    def one_block(query_part):
        scores = masked_scores(query_part, keys_all, key_valid, score_scale)
        row_peak = jnp.max(scores, axis=-1, keepdims=True)
        expanded = jnp.exp(scores - row_peak)
        row_total = jnp.sum(expanded, axis=-1, keepdims=True)
        weights_low = (expanded / row_total).astype(jnp.bfloat16)
        context = jnp.einsum(
            "hqk,khd->qhd", weights_low, values_all, preferred_element_type=jnp.float32
        )
        return (context.astype(jnp.bfloat16), (row_peak + jnp.log(row_total))[..., 0])

    contexts, log_sums = lax.map(one_block, query_blocks)
    return (contexts.reshape(queries.shape), log_sums)


def attend_backward(
    queries, keys_all, values_all, length, log_sums, grad_context, score_scale, block_rows
):
    key_count, heads_here, head_size = keys_all.shape
    key_valid = (jnp.arange(key_count) < length)[None, None, :]
    block_count = key_count // block_rows
    query_blocks = queries.reshape(block_count, block_rows, heads_here, head_size)
    grad_blocks = grad_context.reshape(block_count, block_rows, heads_here, head_size)

    def one_block(carry, inputs_one):
        grad_keys, grad_values = carry
        query_part, grad_part, log_part = inputs_one
        scores = masked_scores(query_part, keys_all, key_valid, score_scale)
        weights_full = jnp.exp(scores - log_part[..., None])
        weights_low = weights_full.astype(jnp.bfloat16)
        grad_values = grad_values + jnp.einsum(
            "hqk,qhd->khd", weights_low, grad_part, preferred_element_type=jnp.float32
        )
        grad_weights = jnp.einsum(
            "qhd,khd->hqk", grad_part, values_all, preferred_element_type=jnp.float32
        )
        center = jnp.sum(weights_full * grad_weights, axis=-1, keepdims=True)
        grad_scores = (weights_full * (grad_weights - center)).astype(jnp.bfloat16)
        grad_query = (
            jnp.einsum("hqk,khd->qhd", grad_scores, keys_all, preferred_element_type=jnp.float32)
            * score_scale
        )
        grad_keys = (
            grad_keys
            + jnp.einsum(
                "hqk,qhd->khd", grad_scores, query_part, preferred_element_type=jnp.float32
            )
            * score_scale
        )
        return ((grad_keys, grad_values), grad_query)

    zero_keys = jnp.zeros(keys_all.shape, jnp.float32)
    (grad_keys, grad_values), grad_queries = lax.scan(
        one_block, (zero_keys, zero_keys), (query_blocks, grad_blocks, log_sums)
    )
    grad_queries = grad_queries.reshape(queries.shape)
    return jnp.stack([grad_queries, grad_keys, grad_values], axis=1).astype(jnp.bfloat16)


def shards(
    hidden_in,
    cotangent,
    lengths,
    qkv_weight,
    q_bias,
    v_bias,
    out_weight,
    out_bias,
    norm1_gain,
    norm1_shift,
    up_weight,
    up_bias,
    down_weight,
    down_bias,
    norm2_gain,
    norm2_shift,
):
    (
        w_qkv,
        b_query,
        b_value,
        w_out,
        b_out,
        g_one,
        s_one,
        w_up,
        b_up,
        w_down,
        b_down,
        g_two,
        s_two,
    ) = (
        lax.all_gather(qkv_weight, "dp", axis=0, tiled=True),
        lax.all_gather(q_bias, "dp", axis=0, tiled=True),
        lax.all_gather(v_bias, "dp", axis=0, tiled=True),
        lax.all_gather(out_weight, "dp", axis=0, tiled=True),
        lax.all_gather(out_bias, "dp", axis=0, tiled=True),
        lax.all_gather(norm1_gain, "dp", axis=0, tiled=True),
        lax.all_gather(norm1_shift, "dp", axis=0, tiled=True),
        lax.all_gather(up_weight, "dp", axis=0, tiled=True),
        lax.all_gather(up_bias, "dp", axis=0, tiled=True),
        lax.all_gather(down_weight, "dp", axis=0, tiled=True),
        lax.all_gather(down_bias, "dp", axis=0, tiled=True),
        lax.all_gather(norm2_gain, "dp", axis=0, tiled=True),
        lax.all_gather(norm2_shift, "dp", axis=0, tiled=True),
    )
    groups, local_len, model_width = hidden_in.shape
    seq_parts = lax.axis_size("seq")
    full_len = local_len * seq_parts
    slice_width = model_width // seq_parts
    heads_here = slice_width // HD
    row_count = groups * local_len
    block_rows = min(512, full_len)
    score_scale = HD ** (-0.5)
    token_rows = hidden_in.reshape(row_count, model_width)
    bias_all = jnp.concatenate(
        [
            b_query.astype(jnp.float32),
            jnp.zeros((model_width,), jnp.float32),
            b_value.astype(jnp.float32),
        ]
    )
    projected = (matmul(token_rows, w_qkv) + bias_all).astype(jnp.bfloat16)
    by_heads = lax.all_to_all(
        projected.reshape(groups, local_len, 3, model_width),
        "seq",
        split_axis=3,
        concat_axis=1,
        tiled=True,
    )
    heads_view = by_heads.reshape(groups, full_len, 3, heads_here, HD)

    def forward_one(inputs_one):
        packed, length = inputs_one
        return attend_forward(
            packed[:, 0], packed[:, 1], packed[:, 2], length, score_scale, block_rows
        )

    contexts, log_sums = lax.map(forward_one, (heads_view, lengths))
    returned_ctx = lax.all_to_all(
        contexts.reshape(groups, full_len, slice_width),
        "seq",
        split_axis=1,
        concat_axis=2,
        tiled=True,
    )
    ctx_rows = returned_ctx.reshape(row_count, model_width)
    attended = matmul(ctx_rows, w_out) + b_out.astype(jnp.float32)
    first_norm, first_back = jax.vjp(
        norm_rows,
        token_rows.astype(jnp.float32) + attended,
        g_one.astype(jnp.float32),
        s_one.astype(jnp.float32),
    )
    first_low = first_norm.astype(jnp.bfloat16)
    pre_act = matmul(first_low, w_up) + b_up.astype(jnp.float32)
    activated, gelu_back = jax.vjp(gelu_exact, pre_act)
    active_low = activated.astype(jnp.bfloat16)
    branch = matmul(active_low, w_down) + b_down.astype(jnp.float32)
    result, second_back = jax.vjp(
        norm_rows, first_norm + branch, g_two.astype(jnp.float32), s_two.astype(jnp.float32)
    )
    back_qkv, back_out, back_up, back_down = (
        lax.all_gather(qkv_weight, "dp", axis=0, tiled=True),
        lax.all_gather(out_weight, "dp", axis=0, tiled=True),
        lax.all_gather(up_weight, "dp", axis=0, tiled=True),
        lax.all_gather(down_weight, "dp", axis=0, tiled=True),
    )
    grad_result = cotangent.reshape(row_count, model_width).astype(jnp.float32)
    grad_second, grad_g_two, grad_s_two = second_back(grad_result)
    grad_branch = grad_second.astype(jnp.bfloat16)
    grad_down_bias = jnp.sum(grad_branch.astype(jnp.float32), axis=0)
    grad_down = inner_rows(active_low, grad_branch)
    (grad_inner,) = gelu_back(inner_cols(grad_branch, back_down))
    grad_pre = grad_inner.astype(jnp.bfloat16)
    grad_up_bias = jnp.sum(grad_pre.astype(jnp.float32), axis=0)
    grad_up = inner_rows(first_low, grad_pre)
    grad_first = grad_second + inner_cols(grad_pre, back_up)
    grad_mid, grad_g_one, grad_s_one = first_back(grad_first)
    grad_attended = grad_mid.astype(jnp.bfloat16)
    grad_out_bias = jnp.sum(grad_attended.astype(jnp.float32), axis=0)
    grad_out = inner_rows(ctx_rows, grad_attended)
    grad_ctx = inner_cols(grad_attended, back_out).astype(jnp.bfloat16)
    grad_heads = lax.all_to_all(
        grad_ctx.reshape(groups, local_len, model_width),
        "seq",
        split_axis=2,
        concat_axis=1,
        tiled=True,
    )
    grad_heads = grad_heads.reshape(groups, full_len, heads_here, HD)

    def backward_one(inputs_one):
        packed, length, log_part, grad_part = inputs_one
        return attend_backward(
            packed[:, 0],
            packed[:, 1],
            packed[:, 2],
            length,
            log_part,
            grad_part,
            score_scale,
            block_rows,
        )

    grad_packed = lax.map(backward_one, (heads_view, lengths, log_sums, grad_heads))
    returned = lax.all_to_all(
        grad_packed.reshape(groups, full_len, 3, slice_width),
        "seq",
        split_axis=1,
        concat_axis=3,
        tiled=True,
    )
    grad_proj = returned.reshape(row_count, 3 * model_width)
    grad_qkv = inner_rows(token_rows, grad_proj)
    bias_sums = jnp.sum(grad_proj.astype(jnp.float32), axis=0)
    grad_q_bias = bias_sums[:model_width]
    grad_v_bias = bias_sums[2 * model_width :]
    grad_input = grad_mid + inner_cols(grad_proj, back_qkv)
    (
        sh_qkv,
        sh_qbias,
        sh_vbias,
        sh_out,
        sh_obias,
        sh_gone,
        sh_sone,
        sh_up,
        sh_ubias,
        sh_down,
        sh_dbias,
        sh_gtwo,
        sh_stwo,
    ) = (
        lax.psum_scatter(grad_qkv, "dp", scatter_dimension=0, tiled=True),
        lax.psum_scatter(grad_q_bias, "dp", scatter_dimension=0, tiled=True),
        lax.psum_scatter(grad_v_bias, "dp", scatter_dimension=0, tiled=True),
        lax.psum_scatter(grad_out, "dp", scatter_dimension=0, tiled=True),
        lax.psum_scatter(grad_out_bias, "dp", scatter_dimension=0, tiled=True),
        lax.psum_scatter(grad_g_one, "dp", scatter_dimension=0, tiled=True),
        lax.psum_scatter(grad_s_one, "dp", scatter_dimension=0, tiled=True),
        lax.psum_scatter(grad_up, "dp", scatter_dimension=0, tiled=True),
        lax.psum_scatter(grad_up_bias, "dp", scatter_dimension=0, tiled=True),
        lax.psum_scatter(grad_down, "dp", scatter_dimension=0, tiled=True),
        lax.psum_scatter(grad_down_bias, "dp", scatter_dimension=0, tiled=True),
        lax.psum_scatter(grad_g_two, "dp", scatter_dimension=0, tiled=True),
        lax.psum_scatter(grad_s_two, "dp", scatter_dimension=0, tiled=True),
    )
    summed = (
        lax.psum(sh_qkv.astype(jnp.bfloat16), "seq").astype(jnp.float32),
        lax.psum(sh_qbias.astype(jnp.bfloat16), "seq").astype(jnp.float32),
        lax.psum(sh_vbias.astype(jnp.bfloat16), "seq").astype(jnp.float32),
        lax.psum(sh_out.astype(jnp.bfloat16), "seq").astype(jnp.float32),
        lax.psum(sh_obias.astype(jnp.bfloat16), "seq").astype(jnp.float32),
        lax.psum(sh_gone.astype(jnp.bfloat16), "seq").astype(jnp.float32),
        lax.psum(sh_sone.astype(jnp.bfloat16), "seq").astype(jnp.float32),
        lax.psum(sh_up.astype(jnp.bfloat16), "seq").astype(jnp.float32),
        lax.psum(sh_ubias.astype(jnp.bfloat16), "seq").astype(jnp.float32),
        lax.psum(sh_down.astype(jnp.bfloat16), "seq").astype(jnp.float32),
        lax.psum(sh_dbias.astype(jnp.bfloat16), "seq").astype(jnp.float32),
        lax.psum(sh_gtwo.astype(jnp.bfloat16), "seq").astype(jnp.float32),
        lax.psum(sh_stwo.astype(jnp.bfloat16), "seq").astype(jnp.float32),
    )
    return (
        result.astype(jnp.bfloat16).reshape(hidden_in.shape),
        grad_input.astype(jnp.bfloat16).reshape(hidden_in.shape),
        summed[0],
        summed[1],
        summed[2],
        summed[3],
        summed[4],
        summed[5],
        summed[6],
        summed[7],
        summed[8],
        summed[9],
        summed[10],
        summed[11],
        summed[12],
    )


def solution(mesh):
    placed = (
        P("dp", "seq", None),
        P("dp", "seq", None),
        P("dp"),
        P("dp", None),
        P("dp"),
        P("dp"),
        P("dp", None),
        P("dp"),
        P("dp"),
        P("dp"),
        P("dp", None),
        P("dp"),
        P("dp", None),
        P("dp"),
        P("dp"),
        P("dp"),
    )
    return jax.shard_map(
        shards,
        mesh=mesh,
        in_specs=placed,
        out_specs=(
            P("dp", "seq", None),
            P("dp", "seq", None),
            P("dp", None),
            P("dp"),
            P("dp"),
            P("dp", None),
            P("dp"),
            P("dp"),
            P("dp"),
            P("dp", None),
            P("dp"),
            P("dp", None),
            P("dp"),
            P("dp"),
            P("dp"),
        ),
        check_vma=False,
    )
```

profile of v0, /device:TPU:0, one launch (start us, length us, event | category | flops | bytes accessed | tf_op | source)
XLA Modules:
  0.0 1070.7 jit_solution(13931852713302982289)
XLA Ops:
  16.6 40.2 %all-reduce.18 = (bf16[768]{0:T(1024)(128)(2,1)S(1)}, bf16[768]{0:T(1024)(128)(2,1)S(1)}, bf16[768]{0:T(1024)(128)(2,1)}, bf16[768]{0:T(1024)(128)(2,1)}, bf16[7...) all-reduce(bf16[768]{0:T(1024)(128)(2,1)S(1)} %dynamic-update-slice, ...), channel_id=1, replica_groups=mesh['dp'=8,'seq'=4] {'dp'}, use_global_device_ids=true, to_apply=%add.1 | all-reduce | flops 6144 | bytes 24576
  56.9 21.7 %all-gather.6.cloned.1.call-done = bf16[768,2304]{1,0:T(8,128)(2,1)} async-done(((bf16[96,2304]{1,0:T(8,128)(2,1)}), bf16[768,2304]{1,0:T(8,128)(2,1)}) %all-gather.6.cloned.1.call-update) | async-done | bytes 3538960 | tf_op jit(solution)/shard_map/all_gather | solution.py:144
  78.5 8.5 add_convert_fusion.1
  87.1 11.3 %reshape.291 = bf16[2,512,3,768]{3,2,1,0:T(4,128)(2,1)} reshape(bf16[1024,2304]{1,0:T(8,128)(2,1)} %add_convert_fusion.1) | data formatting | bytes 9437184 | tf_op jit(solution)/shard_map/reshape | solution.py:176
  98.3 16.4 %copy.108 = bf16[2,512,3,768]{1,0,2,3:T(2,128)(2,1)} copy(bf16[2,512,3,768]{3,2,1,0:T(4,128)(2,1)} %reshape.291) | data formatting | bytes 9437184 | tf_op jit(solution)/shard_map/reshape | solution.py:176
  121.2 52.3 %all-to-all-done = bf16[2,512,3,768]{1,0,2,3:T(2,128)(2,1)} async-done(((bf16[2,512,3,768]{1,0,2,3:T(2,128)(2,1)}), bf16[2,512,3,768]{1,0,2,3:T(2,128)(2,1)}, u32[]{:S(2)}, u32[]{:S(2)}) %all-to-all-start) | async-done | bytes 4718624 | tf_op jit(solution)/shard_map/all_to_all | solution.py:175
  182.5 8.8 reshape.238
  191.2 97.8 %while.51 = (s32[]{:T(128)}, bf16[2,2048,3,64]{1,3,2,0:T(8,128)(2,1)}, f32[2,4,3,512]{3,2,1,0:T(4,128)}, bf16[2,2048,3,3,64]{1,4,3,2,0:T(8,128)(2,1)}, s32[2]{0:T(128)}, /*index=5*/s32[]{:T(128)}, s32[]{:T(128)}, s32[]{:T(128)}) while((s32[]{:T(128)}, bf16[2,2048,3,64]{1,3,2,0:T(8,128)(2,1)}, f32[2,4,3,512]{3,2,1,0:T(4,128)}, ...), condition=%wide.region_5.6_spmd, body=%wide.region_0.5_spmd.sunk | while | flops 843153920 | bytes 57137448 | solution.py:190
  195.3 39.3 %while.54 = (s32[]{:T(128)}, bf16[4,512,3,64]{1,3,2,0:T(8,128)(2,1)}, f32[4,3,512]{2,1,0:T(4,128)S(1)}, bf16[4,512,3,64]{1,3,2,0:T(8,128)(2,1)S(1)}, bf16[2048,3...) while((s32[]{:T(128)}, ...), condition=%wide.region_4.4_spmd.clone, body=%wide.region_1.3_spmd.clone.sunk | while | flops 843153920 | bytes 39778412 | solution.py:63
  244.2 39.3 %while.54 = (s32[]{:T(128)}, bf16[4,512,3,64]{1,3,2,0:T(8,128)(2,1)}, f32[4,3,512]{2,1,0:T(4,128)S(1)}, bf16[4,512,3,64]{1,3,2,0:T(8,128)(2,1)S(1)}, bf16[2048,3...) while((s32[]{:T(128)}, ...), condition=%wide.region_4.4_spmd.clone, body=%wide.region_1.3_spmd.clone.sunk | while | flops 843153920 | bytes 39778412 | solution.py:63
  299.6 26.6 %all-gather = bf16[8,1,384]{2,1,0:T(2,128)(2,1)S(1)} all-gather(bf16[1,1,384]{2,1,0:T(2,128)(2,1)S(1)} %reshape.272), channel_id=1, replica_groups=mesh['dp'=8,'seq'=4] {'dp'}, dimensions={0}, use_global_device_ids=true | all-gather | bytes 6912 | tf_op jit(solution)/shard_map/all_gather | solution.py:152
  326.2 6.4 copy.113
  340.5 35.8 %multiply_convert_fusion.1 = (bf16[1024,3072]{1,0:T(8,128)(2,1)}, f32[1024,3072]{1,0:T(8,128)}, f32[1024,3072]{1,0:T(8,128)}) fusion(f32[3072]{0:T(1024)S(1)} %bitcast.230, bf16[768,3072]{1,0:T(8,128)(2,1)} %all-gather.10.cloned.1.call-done, f32[1024,768]{1,0:T(8,128)S(1)} %get-tuple-element.517, f32[768]{0:T(1024)S(1)} %convert_element_type.186, ...), kind=kOutput, calls=%fused_computation.68 | convolution fusion | flops 5043388416 | bytes 39348224 | tf_op jit(solution)/shard_map/dot_general | solution.py:23
  380.9 8.9 fusion.69
  396.8 18.9 %convert_reduce_fusion = (f32[3072]{0:T(1024)}, bf16[1024,3072]{1,0:T(8,128)(2,1)}) fusion(f32[1024,3072]{1,0:T(8,128)} %get-tuple-element.498, bf16[1024,768]{1,0:T(8,128)(2,1)} %get-tuple-element.490, bf16[3072,768]{1,0:T(8,128)(2,1)} %all-gather.12.cloned.1.call-done, f32[1024,3072]{1,0:T(8,128)} %get-tuple-element.518, f32[3072]{0:T(1024)S(1)} %bitcast.231), kind=kOutput, calls=%fused_computation.66 | convolution fusion | flops 4885312512 | bytes 37773312 | tf_op jit(solution)/shard_map/dot_general | solution.py:33
  415.7 10.1 multiply_reduce_fusion.1
  433.9 10.6 fusion.59
  455.4 10.2 fusion.71
  465.6 9.7 all-to-all-done.2
  479.2 256.1 %while.53 = (s32[]{:T(128)}, bf16[2,2048,3,3,64]{1,4,3,2,0:T(8,128)(2,1)}, bf16[2,2048,3,3,64]{1,4,3,2,0:T(8,128)(2,1)}, bf16[2,2048,3,64]{1,3,2,0:T(8,128)(2,1)...) while((s32[]{:T(128)}, ...), condition=%wide.region_18.19_spmd, body=%wide.region_14.18_spmd.sunk | while | flops 2070381056 | bytes 197102048 | solution.py:257
  492.5 107.1 %while.55 = (s32[]{:T(128)}, f32[2048,3,64]{0,2,1:T(8,128)S(1)}, f32[2048,3,64]{0,2,1:T(8,128)}, bf16[4,512,3,64]{1,3,2,0:T(8,128)(2,1)}, bf16[4,512,3,64]{1,3,2...) while((s32[]{:T(128)}, f32[2048,3,64]{0,2,1:T(8,128)S(1)}, ...), condition=%wide.region_17.17_spmd.clone, body=%wide.region_15.16_spmd.clone.sunk | while | flops 2062516736 | bytes 129419448 | solution.py:104
  620.3 107.3 %while.55 = (s32[]{:T(128)}, f32[2048,3,64]{0,2,1:T(8,128)S(1)}, f32[2048,3,64]{0,2,1:T(8,128)}, bf16[4,512,3,64]{1,3,2,0:T(8,128)(2,1)}, bf16[4,512,3,64]{1,3,2...) while((s32[]{:T(128)}, f32[2048,3,64]{0,2,1:T(8,128)S(1)}, ...), condition=%wide.region_17.17_spmd.clone, body=%wide.region_15.16_spmd.clone.sunk | while | flops 2062516736 | bytes 129419448 | solution.py:104
  735.4 16.1 %copy.117 = bf16[2,2048,3,192]{3,0,2,1:T(2,128)(2,1)} copy(bf16[2,2048,3,192]{1,3,2,0:T(8,128)(2,1)} %bitcast.224) | data formatting | bytes 9437184 | tf_op jit(solution)/shard_map/reshape | solution.py:259
  751.5 77.4 %all_to_all.60 = bf16[2,2048,3,192]{3,0,2,1:T(2,128)(2,1)} all-to-all(bf16[2,2048,3,192]{3,0,2,1:T(2,128)(2,1)} %copy.117), channel_id=1, replica_groups=mesh['dp'=8,'seq'=4] {'seq'}, dimensions={1} | all-to-all | bytes 9437184 | tf_op jit(solution)/shard_map/all_to_all | solution.py:258
  828.9 16.9 %copy.125 = bf16[2,4,512,3,192]{2,1,4,3,0:T(4,128)(2,1)} copy(bf16[2,4,512,3,192]{4,0,3,2,1:T(2,128)(2,1)} %bitcast.216) | data formatting | bytes 9437184 | tf_op jit(solution)/shard_map/all_to_all | solution.py:258
  845.8 9.3 copy.119
  867.1 8.0 copy.126
  881.7 37.7 %all-reduce.17 = (bf16[768]{0:T(1024)(128)(2,1)S(1)}, bf16[768]{0:T(1024)(128)(2,1)S(1)}, bf16[768]{0:T(1024)(128)(2,1)S(1)}, bf16[768]{0:T(1024)(128)(2,1)S(1)}...) all-reduce(f32[768]{0:T(1024)S(1)} %slice.31, ...), channel_id=3, replica_groups=mesh['dp'=8,'seq'=4] {'dp'}, use_global_device_ids=true, to_apply=%region_22.23.clone | all-reduce | flops 9216 | bytes 55296
  920.1 6.2 all-reduce.19
  936.9 66.6 %reduce-scatter.13.cloned.1.call-done = f32[96,2304]{1,0:T(8,128)} async-done(((f32[768,2304]{1,0:T(8,128)}), f32[96,2304]{1,0:T(8,128)}) %reduce-scatter.13.cloned.1.call-update) | async-done | bytes 884752
  1005.8 8.7 add_convert_fusion.2
  1014.5 41.3 %all-reduce.23.cloned.1.call-done = (bf16[96,2304]{0,1:T(8,128)(2,1)}, bf16[96,768]{1,0:T(8,128)(2,1)}, bf16[96,3072]{1,0:T(8,128)(2,1)}, bf16[384,768]{1,0:T(8,128)(2,1)}) async-done(((bf16[96,2304]{0,1:T(8,128)(2,1)}, bf16[96,768]{1,0:T(8,128)(2,1)}, bf16[96,3072]{1,0:T(8,128)(2,1)}, bf16[384,768]{1,0:T(8,128)(2,1)}), (bf16[96,2304]{0,1:T(8,128)(2,1)}, bf16[96,768]{1,0:T(8,128)(2,1)}, ...) | async-done | bytes 1769488 | tf_op jit(solution)/shard_map/psum | solution.py:301
  (353 shorter events, 467.9 us)
Async XLA Ops:
  7.2 71.4 %all-gather.6.cloned.1.call-start = ((), (), s32[]{:S(2)}) async-start(), calls=%async_computation.8 | async-start | bytes 3981312 | tf_op jit(solution)/shard_map/all_gather | solution.py:144
  114.7 58.8 %all-to-all-start = ((bf16[2,512,3,768]{1,0,2,3:T(2,128)(2,1)}), bf16[2,512,3,768]{1,0,2,3:T(2,128)(2,1)}, u32[]{:S(2)}, u32[]{:S(2)}) async-start(bf16[2,512,3,768]{1,0,2,3:T(2,128)(2,1)} %copy.108), calls=%async_computation | async-start | bytes 9437184 | tf_op jit(solution)/shard_map/all_to_all | solution.py:175
  119.7 215.9 %all-gather.8.cloned.1.call-start = ((), (), s32[]{:S(2)}) async-start(), calls=%async_computation.9 | async-start | bytes 1327104 | tf_op jit(solution)/shard_map/all_gather | solution.py:147
  120.4 220.1 %all-gather.10.cloned.1.call-start = ((), (), s32[]{:S(2)}) async-start(), calls=%async_computation.10 | async-start | bytes 5308416 | tf_op jit(solution)/shard_map/all_gather | solution.py:151
  289.1 10.4 copy-start.26
  289.1 10.4 copy-start.25
  289.1 10.4 copy-start.24
  289.1 10.4 copy-start.23
  289.1 10.4 copy-start.22
  289.1 10.5 copy-start.21
  289.1 10.5 copy-start.20
  295.2 31.0 %all-to-all-start.1 = ((bf16[2,2048,192]{2,0,1:T(2,128)(2,1)}), bf16[2,2048,192]{2,0,1:T(2,128)(2,1)S(1)}, u32[]{:S(2)}, u32[]{:S(2)}) async-start(bf16[2,2048,192]{2,0,1:T(2,128)(2,1)} %copy.112), calls=%async_computation.1 | async-start | bytes 4194304 | tf_op jit(solution)/shard_map/all_to_all | solution.py:191
  298.8 82.1 %all-gather.12.cloned.1.call-start = ((), (), s32[]{:S(2)}) async-start(), calls=%async_computation.11 | async-start | bytes 5308416 | tf_op jit(solution)/shard_map/all_gather | solution.py:153
  299.4 631.5 %reduce-scatter.7.cloned.1.call-start = ((), (), s32[]{:S(2)}) async-start(), calls=%async_computation.12 | async-start | bytes 2654208 | tf_op jit(solution)/shard_map/reduce_scatter | solution.py:289
  380.9 9.5 copy-start.1
  433.9 498.7 %reduce-scatter.9.cloned.1.call-start = ((), (), s32[]{:S(2)}) async-start(), calls=%async_computation.13 | async-start | bytes 10616832 | tf_op jit(solution)/shard_map/reduce_scatter | solution.py:293
  448.7 6.7 copy-start.9
  451.7 23.6 %all-to-all-start.2 = ((bf16[2,512,768]{1,0,2:T(2,128)(2,1)}), bf16[2,512,768]{1,0,2:T(2,128)(2,1)S(1)}, u32[]{:S(2)}, u32[]{:S(2)}) async-start(bf16[2,512,768]{1,0,2:T(2,128)(2,1)} %copy.114), calls=%async_computation.2 | async-start | bytes 3145728 | tf_op jit(solution)/shard_map/all_to_all | solution.py:235
  455.3 479.5 %reduce-scatter.11.cloned.1.call-start = ((), (), s32[]{:S(2)}) async-start(), calls=%async_computation.14 | async-start | bytes 10616832 | tf_op jit(solution)/shard_map/reduce_scatter | solution.py:295
  465.6 537.9 %reduce-scatter.13.cloned.1.call-start = ((), (), s32[]{:S(2)}) async-start(), calls=%async_computation.15 | async-start | bytes 7962624
  510.7 5.8 copy-start
  719.4 5.9 copy-start
  855.1 6.2 copy-start.27
  875.2 6.5 copy-start.14
  875.2 6.5 copy-start.15
  875.2 6.5 copy-start.16
  875.2 6.5 copy-start.17
  875.2 6.5 copy-start.18
  875.2 6.5 copy-start.19
  875.2 180.6 %all-reduce.23.cloned.1.call-start = ((), (), s32[]{:S(2)}) async-start(), calls=%async_computation.16 | async-start | bytes 3833856 | tf_op jit(solution)/shard_map/psum | solution.py:301
  881.3 124.5 %copy-start.4 = (f32[1024,768]{1,0:T(8,128)S(1)}, f32[1024,768]{1,0:T(8,128)}, u32[]{:S(2)}) copy-start(f32[1024,768]{1,0:T(8,128)} %copy-done.3) | copy-start | bytes 9437188
  881.3 124.5 %copy-start.13 = (f32[1024]{0:T(1024)S(1)}, f32[1024]{0:T(1024)}, u32[]{:S(2)}) copy-start(f32[1024]{0:T(1024)} %copy-done.12) | copy-start | bytes 12292
  (17 other events, 58.3 us)
Sparse Core Ops, SparseCore 0:
  10.2 68.3 all-gather.5
  122.7 40.1 all-gather.7
  165.1 78.6 all-gather.9
  301.5 79.3 all-gather.11
  434.0 67.2 reduce-scatter.6
  504.7 162.3 reduce-scatter.8
  670.7 162.5 reduce-scatter.10
  875.3 128.2 reduce-scatter.12
  1007.5 48.2 all-reduce.22
where the time goes:
time: 1080 us; the launch traced here: 1070 us
  matrix products  347 us (32%)
  waiting for transfers between devices  199 us (18%)
  local copies, waits for them, and re-layouts  198 us (18%)
  blocking collectives  188 us (17%)
  other arithmetic  108 us (10%)
  between operations  16.7 us (2%)
  starting transfers between devices  12.7 us (1%)
    unnamed x2, blocking collectives  78 us
    all_to_all x1, blocking collectives, shards(): lax.all_to_all(grad_packed.reshape(groups, full_len, 3, slice_width), 'se...  77.4 us
    unnamed x10, waiting for transfers between devices  69.1 us
    dot_general x4, matrix products, matmul(): return jnp.dot(first_op, second_op, preferred_element_type=jnp.float32)  57.7 us
    all_to_all x1, waiting for transfers between devices, shards(): lax.all_to_all(projected.reshape(groups, local_len, 3, model_width), 'seq...  52.3 us
    dot_general x8, matrix products, one_block(): jnp.einsum('hqk,khd->qhd', grad_scores, keys_all, preferred_element_type=...  45.8 us
    dot_general x8, matrix products, one_block(): jnp.einsum('hqk,qhd->khd', weights_low, grad_part, preferred_element_type...  43.6 us
    psum x1, waiting for transfers between devices, shards(): lax.psum(sh_qkv.astype(jnp.bfloat16), 'seq').astype(jnp.float32)  41.3 us
  transfers between devices with their start and end apart: 12, of which 6 were waited for; matrix products, arithmetic and copies ran while one was open for 51% of the time, Pallas kernels for 0%

commit v1 on v0

v1 whole, which is shorter than its diff:
```python
import functools

import jax
import jax.numpy as jnp
from jax import lax
from jax.experimental import pallas as pl
from jax.experimental.pallas import tpu as pltpu
from jax.sharding import PartitionSpec as P

HD = 64


epsilon = 1e-06


def norm_rows(values_in, gain_vec, shift_vec):
    centered = values_in - jnp.mean(values_in, axis=-1, keepdims=True)
    variance = jnp.mean(centered * centered, axis=-1, keepdims=True)
    return centered * lax.rsqrt(variance + epsilon) * gain_vec + shift_vec


def gelu_exact(values_in):
    return jax.nn.gelu(values_in, approximate=False)


def matmul(first_op, second_op):
    return jnp.dot(first_op, second_op, preferred_element_type=jnp.float32)


def inner_rows(first_op, second_op):
    return lax.dot_general(
        first_op, second_op, (((0,), (0,)), ((), ())), preferred_element_type=jnp.float32
    )


def inner_cols(first_op, second_op):
    return lax.dot_general(
        first_op, second_op, (((1,), (1,)), ((), ())), preferred_element_type=jnp.float32
    )


NEG = -1e30


def contract(first_op, second_op, first_dim, second_dim):
    return lax.dot_general(
        first_op,
        second_op,
        (((first_dim,), (second_dim,)), ((), ())),
        preferred_element_type=jnp.float32,
    )


def key_positions(shape, dim, rank, local_len):
    row = lax.broadcasted_iota(jnp.int32, shape, dim)
    return ((row // local_len) ^ rank) * local_len + row % local_len


def fwd_kernel(heads, local_len, meta_ref, q_ref, k_ref, v_ref, ctx_ref, lse_ref):
    length, rank = meta_ref[0], meta_ref[1]
    key_count = k_ref.shape[1]
    valid = key_positions((1, key_count), 1, rank, local_len) < length
    outs = []
    for h in range(heads):
        s = contract(q_ref[h], k_ref[h], 1, 1)
        s = jnp.where(valid, s, NEG)
        m = jnp.max(s, axis=1, keepdims=True)
        e = jnp.exp(s - m)
        total = jnp.sum(e, axis=1, keepdims=True)
        p = (e * (1.0 / total)).astype(jnp.bfloat16)
        outs.append(contract(p, v_ref[h], 1, 0))
        lse_ref[h] = (m + jnp.log(total)).T
    ctx_ref[...] = jnp.concatenate(outs, axis=1).astype(jnp.bfloat16)


def attend_forward(meta, q, k, v, local_len, block_rows):
    heads, key_count, _ = q.shape
    row = pl.BlockSpec((heads, block_rows, HD), lambda i, *_: (0, i, 0))
    full = pl.BlockSpec((heads, key_count, HD), lambda i, *_: (0, 0, 0))
    pairs = heads * key_count * key_count
    return pl.pallas_call(
        functools.partial(fwd_kernel, heads, local_len),
        grid_spec=pltpu.PrefetchScalarGridSpec(
            num_scalar_prefetch=1,
            grid=(key_count // block_rows,),
            in_specs=[row, full, full],
            out_specs=[
                pl.BlockSpec((block_rows, heads * HD), lambda i, *_: (i, 0)),
                pl.BlockSpec((heads, 1, block_rows), lambda i, *_: (0, 0, i)),
            ],
        ),
        out_shape=[
            jax.ShapeDtypeStruct((key_count, heads * HD), jnp.bfloat16),
            jax.ShapeDtypeStruct((heads, 1, key_count), jnp.float32),
        ],
        compiler_params=pltpu.CompilerParams(vmem_limit_bytes=48 << 20),
        cost_estimate=pl.CostEstimate(
            flops=16 * pairs * HD, bytes_accessed=8 * q.size, transcendentals=pairs
        ),
        name="attend_forward",
    )(meta, q, k, v)


def bwd_kernel(
    heads,
    local_len,
    meta_ref,
    q_ref,
    k_ref,
    v_ref,
    do_ref,
    lse_ref,
    dq_ref,
    dk_ref,
    dv_ref,
    dk_acc,
    dv_acc,
):
    length, rank = meta_ref[0], meta_ref[1]
    step = pl.program_id(0)
    key_count = k_ref.shape[1]
    valid = key_positions((key_count, 1), 0, rank, local_len) < length

    @pl.when(step == 0)
    def _():
        dk_acc[...] = jnp.zeros_like(dk_acc)
        dv_acc[...] = jnp.zeros_like(dv_acc)

    dqs = []
    for h in range(heads):
        q = q_ref[h]
        k = k_ref[h]
        do = do_ref[:, h * HD : (h + 1) * HD]
        s = jnp.where(valid, contract(k, q, 1, 1), NEG)
        p = jnp.exp(s - lse_ref[h])
        dv_acc[h] += contract(p.astype(jnp.bfloat16), do, 1, 0)
        gp = contract(v_ref[h], do, 1, 1)
        center = jnp.sum(p * gp, axis=0, keepdims=True)
        ds = (p * (gp - center)).astype(jnp.bfloat16)
        dk_acc[h] += contract(ds, q, 1, 0)
        dqs.append(contract(ds, k, 0, 0) * HD ** (-0.5))
    dq_ref[...] = jnp.concatenate(dqs, axis=1).astype(jnp.bfloat16)

    @pl.when(step == pl.num_programs(0) - 1)
    def _():
        dk_ref[...] = jnp.concatenate([dk_acc[h] for h in range(heads)], axis=1).astype(jnp.bfloat16)
        dv_ref[...] = jnp.concatenate([dv_acc[h] for h in range(heads)], axis=1).astype(jnp.bfloat16)


def attend_backward(meta, q, k, v, do, lse, local_len, block_rows):
    heads, key_count, _ = q.shape
    width = heads * HD
    row = pl.BlockSpec((heads, block_rows, HD), lambda i, *_: (0, i, 0))
    full = pl.BlockSpec((heads, key_count, HD), lambda i, *_: (0, 0, 0))
    flat = pl.BlockSpec((block_rows, width), lambda i, *_: (i, 0))
    flat_full = pl.BlockSpec((key_count, width), lambda i, *_: (0, 0))
    shape = jax.ShapeDtypeStruct((key_count, width), jnp.bfloat16)
    pairs = heads * key_count * key_count
    return pl.pallas_call(
        functools.partial(bwd_kernel, heads, local_len),
        grid_spec=pltpu.PrefetchScalarGridSpec(
            num_scalar_prefetch=1,
            grid=(key_count // block_rows,),
            in_specs=[
                row,
                full,
                full,
                flat,
                pl.BlockSpec((heads, 1, block_rows), lambda i, *_: (0, 0, i)),
            ],
            out_specs=[flat, flat_full, flat_full],
            scratch_shapes=[pltpu.VMEM((heads, key_count, HD), jnp.float32)] * 2,
        ),
        out_shape=[shape, shape, shape],
        compiler_params=pltpu.CompilerParams(vmem_limit_bytes=56 << 20),
        cost_estimate=pl.CostEstimate(
            flops=40 * pairs * HD, bytes_accessed=16 * q.size, transcendentals=pairs
        ),
        name="attend_backward",
    )(meta, q, k, v, do, lse)


def project_kernel(heads, x_ref, w_ref, b_ref, q_ref, k_ref, v_ref):
    out = contract(x_ref[...], w_ref[...], 1, 0) + b_ref[...]
    out = out.astype(jnp.bfloat16)
    for part, ref in enumerate((q_ref, k_ref, v_ref)):
        for h in range(heads):
            at = (part * heads + h) * HD
            cols = out[:, at : at + HD]
            ref[h] = cols * 0.125 if part == 0 else cols


def project(x, w, b, heads, block_rows):
    rows, width = x.shape
    out = pl.BlockSpec((heads, block_rows, HD), lambda i: (0, i, 0))
    shape = jax.ShapeDtypeStruct((heads, rows, HD), jnp.bfloat16)
    return pl.pallas_call(
        functools.partial(project_kernel, heads),
        grid=(rows // block_rows,),
        in_specs=[
            pl.BlockSpec((block_rows, width), lambda i: (i, 0)),
            pl.BlockSpec(w.shape, lambda i: (0, 0)),
            pl.BlockSpec(b.shape, lambda i: (0, 0)),
        ],
        out_specs=[out, out, out],
        out_shape=[shape, shape, shape],
        compiler_params=pltpu.CompilerParams(vmem_limit_bytes=32 << 20),
        cost_estimate=pl.CostEstimate(
            flops=2 * rows * width * w.shape[1], bytes_accessed=4 * x.size, transcendentals=0
        ),
        name="project",
    )(x, w, b)


def swap(values, bits):
    pairs = [(r, r ^ bits) for r in range(4)]
    return lax.ppermute(values, "seq", pairs)


def xor_order(values, rank, dim):
    size = values.shape[dim] // 4
    return jnp.concatenate(
        [lax.dynamic_slice_in_dim(values, (rank ^ j) * size, size, dim) for j in range(4)], axis=dim
    )


def seq_sum(values):
    low = values.astype(jnp.bfloat16)
    low = (low.astype(jnp.float32) + swap(low, 1).astype(jnp.float32)).astype(jnp.bfloat16)
    return low.astype(jnp.float32) + swap(low, 2).astype(jnp.float32)


def scatter_sum(values):
    return lax.psum_scatter(values.astype(jnp.bfloat16), "dp", scatter_dimension=0, tiled=True)


def shards(
    hidden_in,
    cotangent,
    lengths,
    qkv_weight,
    q_bias,
    v_bias,
    out_weight,
    out_bias,
    norm1_gain,
    norm1_shift,
    up_weight,
    up_bias,
    down_weight,
    down_bias,
    norm2_gain,
    norm2_shift,
):
    f32, bf16 = jnp.float32, jnp.bfloat16
    rank = lax.axis_index("seq")
    parts = lax.axis_size("dp")
    groups, local_len, width = hidden_in.shape
    own = width // 4
    heads = own // HD
    full_len = 4 * local_len
    row_count = groups * local_len
    shard = width // parts
    wide = 3 * own

    qkv_own = lax.dynamic_slice_in_dim(qkv_weight.reshape(shard, 3, width), rank * own, own, 2)
    qkv_own = qkv_own.reshape(shard, wide)
    smalls = (q_bias, v_bias, out_bias, norm1_gain, norm1_shift, down_bias, norm2_gain, norm2_shift, up_bias)
    small = jnp.concatenate(smalls)
    small_rows = -(-small.size // wide)
    small_rows += (-(shard + small_rows)) % 16
    small = jnp.pad(small, (0, small_rows * wide - small.size)).reshape(small_rows, wide)
    packed = lax.all_gather(jnp.concatenate([qkv_own, small]), "dp", axis=0, tiled=False)

    tokens = []
    for g in range(groups):
        mine = hidden_in[g]
        far = swap(mine, 2)
        both = jnp.stack([mine, far])
        near = swap(both, 1)
        tokens.append(jnp.concatenate([mine, near[0], far, near[1]], axis=0))

    w_out = lax.all_gather(out_weight, "dp", axis=0, tiled=True)
    w_up = lax.all_gather(up_weight, "dp", axis=0, tiled=True)
    w_down = lax.all_gather(down_weight, "dp", axis=0, tiled=True)

    w_own = packed[:, :shard].reshape(width, wide)
    small = packed[:, shard:].reshape(parts, small_rows * wide)
    vectors, at = [], 0
    for vec in smalls:
        vectors.append(small[:, at : at + vec.size].reshape(parts * vec.size).astype(f32))
        at += vec.size
    b_query, b_value, b_out, g_one, s_one, b_down, g_two, s_two, b_up = vectors
    bias_own = jnp.concatenate(
        [
            lax.dynamic_slice_in_dim(b_query, rank * own, own),
            jnp.zeros((own,), f32),
            lax.dynamic_slice_in_dim(b_value, rank * own, own),
        ]
    )[None]

    metas, heads_of, contexts = [], [], []
    for g in range(groups):
        meta = jnp.stack([lengths[g], rank.astype(jnp.int32)])
        q, k, v = project(tokens[g], w_own, bias_own, heads, local_len)
        ctx, lse = attend_forward(meta, q, k, v, local_len, local_len // 2)
        chunks = [ctx[j * local_len : (j + 1) * local_len] for j in range(4)]
        got = [chunks[0]] + [swap(chunks[j], j) for j in (1, 2, 3)]
        contexts.append(jnp.concatenate(got, axis=1))
        metas.append(meta)
        heads_of.append((q, k, v, lse))

    token_rows = hidden_in.reshape(row_count, width)
    ctx_rows = jnp.concatenate(contexts, axis=0)
    w_out = xor_order(w_out, rank, 0)
    attended = matmul(ctx_rows, w_out) + b_out
    first_norm, first_back = jax.vjp(norm_rows, token_rows.astype(f32) + attended, g_one, s_one)
    first_low = first_norm.astype(bf16)
    pre_act = matmul(first_low, w_up) + b_up
    activated, gelu_back = jax.vjp(gelu_exact, pre_act)
    active_low = activated.astype(bf16)
    branch = matmul(active_low, w_down) + b_down
    result, second_back = jax.vjp(norm_rows, first_norm + branch, g_two, s_two)
    grad_result = cotangent.reshape(row_count, width).astype(f32)
    grad_second, grad_g_two, grad_s_two = second_back(grad_result)
    grad_branch = grad_second.astype(bf16)
    grad_down_bias = jnp.sum(grad_branch.astype(f32), axis=0)
    sh_down = scatter_sum(inner_rows(active_low, grad_branch))
    (grad_inner,) = gelu_back(inner_cols(grad_branch, w_down))
    grad_pre = grad_inner.astype(bf16)
    grad_up_bias = jnp.sum(grad_pre.astype(f32), axis=0)
    sh_up = scatter_sum(inner_rows(first_low, grad_pre))
    grad_first = grad_second + inner_cols(grad_pre, w_up)
    grad_mid, grad_g_one, grad_s_one = first_back(grad_first)
    grad_attended = grad_mid.astype(bf16)
    grad_out_bias = jnp.sum(grad_attended.astype(f32), axis=0)
    grad_ctx = inner_cols(grad_attended, w_out).astype(bf16).reshape(groups, local_len, 4, own)
    grad_out = xor_order(inner_rows(ctx_rows, grad_attended), rank, 0)
    rest = (grad_out_bias, grad_g_one, grad_s_one, grad_down_bias, grad_g_two, grad_s_two, grad_up_bias)
    rest_all = jnp.concatenate([vec.reshape(parts, -1) for vec in rest], axis=1).astype(bf16)
    rest_rows = -(-rest_all.shape[1] // width)
    rest_rows += (-(shard + rest_rows)) % 16
    rest_all = jnp.pad(rest_all, ((0, 0), (0, rest_rows * width - rest_all.shape[1])))
    out_all = jnp.concatenate(
        [grad_out.astype(bf16).reshape(parts, shard, width), rest_all.reshape(parts, rest_rows, width)], axis=1
    )
    sh_out = scatter_sum(out_all.reshape(parts * (shard + rest_rows), width))

    grad_qkv = jnp.zeros((width, wide), f32)
    bias_sums = jnp.zeros((wide,), f32)
    grad_inputs = []
    for g in range(groups):
        q, k, v, lse = heads_of[g]
        do = [grad_ctx[g, :, 0]] + [swap(grad_ctx[g, :, j], j) for j in (1, 2, 3)]
        do = jnp.concatenate(do, axis=0)
        grads = attend_backward(metas[g], q, k, v, do, lse, local_len, local_len)
        grad_proj = jnp.concatenate(grads, axis=1)
        part = inner_cols(grad_proj, w_own).reshape(4, local_len, width)
        near = swap(part[1::2].astype(bf16), 1).astype(f32)
        far = swap((part[2] + near[1]).astype(bf16), 2).astype(f32)
        mid = grad_mid[g * local_len : (g + 1) * local_len]
        grad_inputs.append((mid + part[0] + near[0] + far).astype(bf16))
        grad_qkv = grad_qkv + inner_rows(tokens[g], grad_proj)
        bias_sums = bias_sums + jnp.sum(grad_proj.astype(f32), axis=0)

    bias_full = jnp.zeros((2, width), f32)
    bias_full = lax.dynamic_update_slice(bias_full, bias_sums[None, :own], (0, rank * own))
    bias_full = lax.dynamic_update_slice(bias_full, bias_sums[None, 2 * own :], (1, rank * own))
    bias_full = bias_full.reshape(2, parts, shard).transpose(1, 0, 2).reshape(parts, 2 * shard)
    bias_rows = -(-2 * shard // wide)
    bias_rows += (-(shard + bias_rows)) % 16
    bias_full = jnp.pad(bias_full, ((0, 0), (0, bias_rows * wide - 2 * shard)))
    qkv_all = jnp.concatenate(
        [grad_qkv.reshape(parts, shard, wide), bias_full.reshape(parts, bias_rows, wide)], axis=1
    )
    sh_qkv = scatter_sum(qkv_all.reshape(parts * (shard + bias_rows), wide))
    far = swap(sh_qkv, 2)
    both = jnp.stack([sh_qkv, far])
    near = swap(both, 1)
    four = jnp.concatenate([sh_qkv, near[0], far, near[1]], axis=0)
    four = xor_order(four, rank, 0).reshape(4, shard + bias_rows, wide).astype(f32)
    out_qkv = four[:, :shard].reshape(4, shard, 3, own).transpose(1, 2, 0, 3).reshape(shard, 3 * width)
    biases = jnp.sum(four[:, shard:].reshape(4, bias_rows * wide), axis=0)

    out_down = seq_sum(sh_down)
    out_up = seq_sum(sh_up)
    out_out = seq_sum(sh_out)
    flat = out_out[shard:].reshape(-1)
    finals, at = [], 0
    for vec in rest:
        size = vec.size // parts
        finals.append(flat[at : at + size])
        at += size
    o_bias, o_gone, o_sone, o_dbias, o_gtwo, o_stwo, o_ubias = finals
    return (
        result.astype(bf16).reshape(hidden_in.shape),
        jnp.stack(grad_inputs),
        out_qkv,
        biases[:shard],
        biases[shard : 2 * shard],
        out_out[:shard],
        o_bias,
        o_gone,
        o_sone,
        out_up,
        o_ubias,
        out_down,
        o_dbias,
        o_gtwo,
        o_stwo,
    )


def solution(mesh):
    placed = (
        P("dp", "seq", None),
        P("dp", "seq", None),
        P("dp"),
        P("dp", None),
        P("dp"),
        P("dp"),
        P("dp", None),
        P("dp"),
        P("dp"),
        P("dp"),
        P("dp", None),
        P("dp"),
        P("dp", None),
        P("dp"),
        P("dp"),
        P("dp"),
    )
    return jax.shard_map(
        shards,
        mesh=mesh,
        in_specs=placed,
        out_specs=(
            P("dp", "seq", None),
            P("dp", "seq", None),
            P("dp", None),
            P("dp"),
            P("dp"),
            P("dp", None),
            P("dp"),
            P("dp"),
            P("dp"),
            P("dp", None),
            P("dp"),
            P("dp", None),
            P("dp"),
            P("dp"),
            P("dp"),
        ),
        check_vma=False,
    )
```

time: 1080 us -> 800 us (0.74)
  matrix products: 347 us -> 127 us
  Pallas kernels: 0 us -> 162 us
  local copies, waits for them, and re-layouts: 198 us -> 40.3 us
  blocking collectives: 188 us -> 36.4 us
  waiting for transfers between devices: 199 us -> 336 us
  other arithmetic: 108 us -> 55.9 us
    reduce_scatter x3 -> x4, waiting for transfers between devices: 0.01 us -> 239 us  [scatter_sum(): lax.psum_scatter(values.astype(jnp.bfloat16), 'dp', scatter_dimension=0,...]
    dot_general x56 -> x0, matrix products: 220 us -> none  [the longest x8 45.8 us: one_block(): jnp.einsum('hqk,khd->qhd', grad_scores, keys_all, preferred_element_type=...]
    pallas_call x0 -> x6, Pallas kernels: none -> 162 us  [the longest x2 98.3 us: attend_backward(): pl.pallas_call(functools.partial(bwd_kernel, heads, local_len), grid_spec...]
    ppermute x0 -> x28, waiting for transfers between devices: none -> 82.2 us  [swap(): return lax.ppermute(values, 'seq', pairs)]
    unnamed x2 -> x0, blocking collectives: 78 us -> none
    all_to_all x1 -> x0, blocking collectives: 77.4 us -> none  [shards(): lax.all_to_all(grad_packed.reshape(groups, full_len, 3, slice_width), 'se...]
    unnamed x10 -> x7, waiting for transfers between devices: 69.1 us -> 1.46 us
    all_to_all x3 -> x0, waiting for transfers between devices: 62 us -> none  [the longest x1 52.3 us: shards(): lax.all_to_all(projected.reshape(groups, local_len, 3, model_width), 'seq...]
  transfers between devices with their start and end apart: 12 -> 35, of which waited for: 6 -> 14; matrix products, arithmetic and copies ran while one was open for 51% -> 17% of each run, Pallas kernels for 0% -> 14%
where the time goes in v1:
time: 800 us; the launch traced here: 796 us
  waiting for transfers between devices  336 us (42%)
  Pallas kernels  162 us (20%)
  matrix products  127 us (16%)
  other arithmetic  55.9 us (7%)
  local copies, waits for them, and re-layouts  40.3 us (5%)
  blocking collectives  36.4 us (5%)
  starting transfers between devices  22.8 us (3%)
  between operations  15.7 us (2%)
    reduce_scatter x4, waiting for transfers between devices, scatter_sum(): lax.psum_scatter(values.astype(jnp.bfloat16), 'dp', scatter_dimension=0,...  239 us
    pallas_call x2, Pallas kernels, attend_backward(): pl.pallas_call(functools.partial(bwd_kernel, heads, local_len), grid_spec...  98.3 us
    ppermute x28, waiting for transfers between devices, swap(): return lax.ppermute(values, 'seq', pairs)  82.2 us
    pallas_call x2, Pallas kernels, attend_forward(): pl.pallas_call(functools.partial(fwd_kernel, heads, local_len), grid_spec...  56.5 us
    dot_general x3, matrix products, matmul(): return jnp.dot(first_op, second_op, preferred_element_type=jnp.float32)  52.1 us
    dot_general x5, matrix products, inner_cols(): lax.dot_general(first_op, second_op, (((1,), (1,)), ((), ())), preferred_...  39.7 us
    all_gather x1, blocking collectives, shards(): lax.all_gather(jnp.concatenate([qkv_own, small]), 'dp', axis=0, tiled=False)  36.4 us
    dot_general x5, matrix products, inner_rows(): lax.dot_general(first_op, second_op, (((0,), (0,)), ((), ())), preferred_...  35.7 us
  transfers between devices with their start and end apart: 35, of which 14 were waited for; matrix products, arithmetic and copies ran while one was open for 17% of the time, Pallas kernels for 14%

profile of v1, /device:TPU:0, one launch (start us, length us, event | category | flops | bytes accessed | tf_op | source)
XLA Modules:
  0.0 796.2 jit_solution(15277234418779259306)
XLA Ops:
  14.3 17.5 %collective-permute-done = bf16[512,768]{1,0:T(8,128)(2,1)S(1)} collective-permute-done((bf16[512,768]{1,0:T(8,128)(2,1)S(1)}, bf16[512,768]{1,0:T(8,128)(2,1)S(1)}, u32[]{:S(2)}, u32[]{:S(2)}) %collective-permute-start) | collective-permute-done | bytes 786464 | tf_op jit(solution)/shard_map/ppermute | solution.py:217
  37.7 36.4 %all-gather = bf16[896,576]{1,0:T(8,128)(2,1)S(1)} all-gather(bf16[112,576]{1,0:T(8,128)(2,1)S(1)} %copy.67), channel_id=2, replica_groups=mesh['dp'=8,'seq'=4] {'dp'}, dimensions={0}, use_global_device_ids=true | all-gather | bytes 1161216 | tf_op jit(solution)/shard_map/all_gather | solution.py:273
  86.3 28.0 %attend_forward.2 = (bf16[2048,192]{1,0:T(8,128)(2,1)S(1)}, f32[3,1,2048]{2,1,0:T(1,128)S(1)}) custom-call(s32[2]{0:T(128)S(1)} %get-tuple-element.135.meta_ref, bf16[3,2048,64]{2,1,0:T(8,128)(2,1)S(1)} %get-tuple-element.31.q_ref, bf16[3,2048,64]{2,1,0:T(8,128)(2,1)S(1)} %get-tuple-element.32.k_ref, bf16[3,2048,64]{2,1,0:T(8,128)(2,1)S(1)} %get-tuple-element.33.v_ref), custom_call_target="tpu_custom_call" | custom-call | flops 12884901888 | bytes 3145728 | tf_op jit(solution)/shard_map/attend_forward/pallas_call | solution.py:81
  117.2 6.3 pad_maximum_fusion.1.x_ref
  127.2 28.5 %attend_forward.3 = (bf16[2048,192]{1,0:T(8,128)(2,1)S(1)}, f32[3,1,2048]{2,1,0:T(1,128)S(1)}) custom-call(s32[2]{0:T(128)S(1)} %get-tuple-element.136.meta_ref, bf16[3,2048,64]{2,1,0:T(8,128)(2,1)S(1)} %get-tuple-element.35.q_ref, bf16[3,2048,64]{2,1,0:T(8,128)(2,1)S(1)} %get-tuple-element.36.k_ref, bf16[3,2048,64]{2,1,0:T(8,128)(2,1)S(1)} %get-tuple-element.37.v_ref), custom_call_target="tpu_custom_call" | custom-call | flops 12884901888 | bytes 3145728 | tf_op jit(solution)/shard_map/attend_forward/pallas_call | solution.py:81
  162.0 4.8 collective-permute-done.8
  170.7 4.6 fusion.48
  177.7 38.1 %multiply_convert_fusion = (bf16[1024,3072]{1,0:T(8,128)(2,1)}, f32[1024,3072]{1,0:T(8,128)}, f32[1024,3072]{1,0:T(8,128)}) fusion(f32[3072]{0:T(1024)S(1)} %reshape.299, bf16[768,3072]{1,0:T(8,128)(2,1)} %all-gather.7.cloned.1.call-done, f32[1024,768]{1,0:T(8,128)} %get-tuple-element.124, f32[768]{0:T(1024)S(1)} %reshape.298, f32[768]{0:T(1024)S(1)} %reshape.297, ...), kind=kOutput, calls=%fused_computation.3 | convolution fusion | flops 5043388416 | bytes 39348224 | tf_op jit(solution)/shard_map/dot_general | solution.py:27
  215.8 12.6 %all-gather.9.cloned.1.call-done = bf16[3072,768]{1,0:T(8,128)(2,1)} async-done(((bf16[384,768]{1,0:T(8,128)(2,1)}), bf16[3072,768]{1,0:T(8,128)(2,1)}) %all-gather.9.cloned.1.call-update) | async-done | bytes 4718608 | tf_op jit(solution)/shard_map/all_gather | solution.py:285
  228.4 9.5 %fusion.49 = (f32[1024]{0:T(1024)S(1)}, f32[1024,768]{1,0:T(8,128)S(1)}) fusion(f32[768]{0:T(1024)S(1)} %reshape.300, bf16[1024,3072]{1,0:T(8,128)(2,1)} %get-tuple-element.60, bf16[3072,768]{1,0:T(8,128)(2,1)} %all-gather.9.cloned.1.call-done, f32[768]{0:T(1024)S(1)} %reshape.298, f32[768]{0:T(1024)S(1)} %reshape.297, f32[1024]{0:T(1024)S(1)} %fusion.23, ...), kind=kOutput, calls=%fused_computation.160 | convolution fusion | flops 4837342208 | bytes 17323008 | tf_op jit(solution)/shard_map/dot_general | solution.py:27
  244.7 17.9 %fusion.52 = (bf16[3072]{0:T(1024)(128)(2,1)}, bf16[1024,3072]{1,0:T(8,128)(2,1)}) fusion(f32[1024,3072]{1,0:T(8,128)} %get-tuple-element.61, bf16[1024,768]{1,0:T(8,128)(2,1)S(1)} %get-tuple-element.53, bf16[3072,768]{1,0:T(8,128)(2,1)} %all-gather.9.cloned.1.call-done, f32[1024,3072]{1,0:T(8,128)} %get-tuple-element.125, f32[3072]{0:T(1024)S(1)} %reshape.299), kind=kOutput, calls=%fused_computation.163 | convolution fusion | flops 4882166784 | bytes 37767168 | tf_op jit(solution)/shard_map/dot_general | solution.py:37
  262.6 10.6 %multiply_reduce_fusion = (bf16[768]{0:T(1024)(128)(2,1)}, f32[1024]{0:T(1024)S(1)}, bf16[768]{0:T(1024)(128)(2,1)}, f32[1024,768]{1,0:T(8,128)S(1)}) fusion(f32[1024,768]{1,0:T(8,128)} %get-tuple-element.124, f32[1024]{0:T(1024)S(1)} %fusion.23, f32[1024]{0:T(1024)S(1)} %broadcast_multiply_fusion.1, f32[768]{0:T(1024)S(1)} %reshape.297, ...), kind=kOutput, calls=%fused_computation.32 | convolution fusion | flops 4839699456 | bytes 20469760 | tf_op jit(solution)/shard_map/dot_general | solution.py:37
  278.9 4.5 convolution_convert_fusion.2
  283.4 4.4 reshape.308
  295.3 4.9 collective-permute-done.16
  300.1 4.8 collective-permute-done.17
  306.1 49.2 %attend_backward.3 = (bf16[2048,192]{1,0:T(8,128)(2,1)}, bf16[2048,192]{1,0:T(8,128)(2,1)}, bf16[2048,192]{1,0:T(8,128)(2,1)}) custom-call(s32[2]{0:T(128)} %copy-done.3, bf16[3,2048,64]{2,1,0:T(8,128)(2,1)} %copy-done.7, bf16[3,2048,64]{2,1,0:T(8,128)(2,1)} %copy-done.8, bf16[3,2048,64]{2,1,0:T(8,128)(2,1)} %copy-done.9, ...), custom_call_target="tpu_custom_call" | custom-call | flops 32212254720 | bytes 6291456 | tf_op jit(solution)/shard_map/attend_backward/pallas_call | solution.py:159
  355.4 5.7 fusion.30
  363.4 49.1 %attend_backward.2 = (bf16[2048,192]{1,0:T(8,128)(2,1)}, bf16[2048,192]{1,0:T(8,128)(2,1)}, bf16[2048,192]{1,0:T(8,128)(2,1)}) custom-call(s32[2]{0:T(128)} %copy-done.2, bf16[3,2048,64]{2,1,0:T(8,128)(2,1)} %copy-done.4, bf16[3,2048,64]{2,1,0:T(8,128)(2,1)} %copy-done.5, bf16[3,2048,64]{2,1,0:T(8,128)(2,1)} %copy-done.6, ...), custom_call_target="tpu_custom_call" | custom-call | flops 32212254720 | bytes 6291456 | tf_op jit(solution)/shard_map/attend_backward/pallas_call | solution.py:159
  415.6 5.4 add_convert_fusion.3
  428.9 9.8 %convolution_convert_fusion = bf16[3072,768]{1,0:T(8,128)(2,1)} fusion(bf16[1024,3072]{1,0:T(8,128)(2,1)} %get-tuple-element.60, bf16[1024,768]{1,0:T(8,128)(2,1)S(1)} %copy-done.23), kind=kOutput, calls=%fused_computation.19 | convolution fusion | flops 4834197504 | bytes 12582912 | tf_op jit(solution)/shard_map/dot_general | solution.py:31
  441.1 4.0 fusion.27
  446.6 10.8 %convolution_convert_fusion.1 = bf16[768,3072]{1,0:T(8,128)(2,1)} fusion(bf16[1024,3072]{1,0:T(8,128)(2,1)} %get-tuple-element.134, f32[1024,768]{1,0:T(8,128)} %get-tuple-element.124, f32[768]{0:T(1024)S(1)} %copy-done.57, f32[768]{0:T(1024)S(1)} %reshape.297, f32[1024]{0:T(1024)S(1)} %copy-done.51, f32[1024]{0:T(1024)S(1)} %broadcast_multiply_fusion.1), kind=kOutput, calls=%fused_computation.20 | convolution fusion | flops 4838129664 | bytes 14170112 | tf_op jit(solution)/shard_map/dot_general | solution.py:31
  459.0 4.0 fusion.51
  479.7 7.7 reduce-scatter.13.cloned.1.call-done
  488.8 23.4 %collective-permute-done.20 = bf16[112,576]{1,0:T(8,128)(2,1)S(1)} collective-permute-done((bf16[112,576]{1,0:T(8,128)(2,1)}, bf16[112,576]{1,0:T(8,128)(2,1)S(1)}, u32[]{:S(2)}, u32[]{:S(2)}) %collective-permute-start.20) | collective-permute-done | bytes 129056 | tf_op jit(solution)/shard_map/ppermute | solution.py:217
  513.3 4.6 fusion.21
  519.4 66.2 %reduce-scatter.11.cloned.1.call-done = bf16[384,768]{1,0:T(8,128)(2,1)} async-done(((bf16[3072,768]{1,0:T(8,128)(2,1)}), bf16[384,768]{1,0:T(8,128)(2,1)}) %reduce-scatter.11.cloned.1.call-update) | async-done | bytes 589840 | tf_op jit(solution)/shard_map/reduce_scatter | solution.py:234
  585.8 67.5 %reduce-scatter.7.cloned.1.call-done = bf16[112,768]{1,0:T(8,128)(2,1)} async-done(((bf16[896,768]{1,0:T(8,128)(2,1)}), bf16[112,768]{1,0:T(8,128)(2,1)}) %reduce-scatter.7.cloned.1.call-update) | async-done | bytes 172048 | tf_op jit(solution)/shard_map/reduce_scatter | solution.py:234
  653.4 97.9 %reduce-scatter.9.cloned.1.call-done = bf16[96,3072]{1,0:T(8,128)(2,1)} async-done(((bf16[768,3072]{1,0:T(8,128)(2,1)}), bf16[96,3072]{1,0:T(8,128)(2,1)}) %reduce-scatter.9.cloned.1.call-update) | async-done | bytes 589840 | tf_op jit(solution)/shard_map/reduce_scatter | solution.py:234
  765.2 10.6 %collective-permute-done.27 = bf16[384,768]{1,0:T(8,128)(2,1)S(1)} collective-permute-done((bf16[384,768]{1,0:T(8,128)(2,1)S(1)}, bf16[384,768]{1,0:T(8,128)(2,1)S(1)}, u32[]{:S(2)}, u32[]{:S(2)}) %collective-permute-start.27) | collective-permute-done | bytes 589856 | tf_op jit(solution)/shard_map/ppermute | solution.py:217
  776.9 11.1 %collective-permute-done.25 = bf16[96,3072]{1,0:T(8,128)(2,1)S(1)} collective-permute-done((bf16[96,3072]{1,0:T(8,128)(2,1)S(1)}, bf16[96,3072]{1,0:T(8,128)(2,1)S(1)}, u32[]{:S(2)}, u32[]{:S(2)}) %collective-permute-start.25) | collective-permute-done | bytes 589856 | tf_op jit(solution)/shard_map/ppermute | solution.py:217
  (338 shorter events, 120.3 us)
Async XLA Ops:
  7.2 153.5 %all-gather.5.cloned.1.call-start = ((), (), s32[]{:S(2)}) async-start(), calls=%async_computation.4 | async-start | bytes 1327104 | tf_op jit(solution)/shard_map/all_gather | solution.py:283
  7.9 169.8 %all-gather.7.cloned.1.call-start = ((), (), s32[]{:S(2)}) async-start(), calls=%async_computation.5 | async-start | bytes 5308416 | tf_op jit(solution)/shard_map/all_gather | solution.py:284
  8.7 219.7 %all-gather.9.cloned.1.call-start = ((), (), s32[]{:S(2)}) async-start(), calls=%async_computation.6 | async-start | bytes 5308416 | tf_op jit(solution)/shard_map/all_gather | solution.py:285
  11.2 20.6 %collective-permute-start = (bf16[512,768]{1,0:T(8,128)(2,1)S(1)}, bf16[512,768]{1,0:T(8,128)(2,1)S(1)}, u32[]{:S(2)}, u32[]{:S(2)}) collective-permute-start(bf16[512,768]{1,0:T(8,128)(2,1)S(1)} %get-tuple-element.76), channel_id=1, source_target_pairs={{0,2},{1,3},{2,0},{3,1},{4,6},{5,7},{6,4},{7,5},{8,10},{9,11},{10,... | collective-permute-start | bytes 2359304 | tf_op jit(solution)/shard_map/ppermute | solution.py:217
  33.2 46.7 %collective-permute-start.1 = (bf16[2,512,768]{2,1,0:T(8,128)(2,1)}, bf16[2,512,768]{2,1,0:T(8,128)(2,1)}, u32[]{:S(2)}, u32[]{:S(2)}) collective-permute-start(bf16[2,512,768]{2,1,0:T(8,128)(2,1)} %pad_maximum_fusion.4), channel_id=1, source_target_pairs={{0,1},{1,0},{2,3},{3,2},{4,5},{5,4},{6,7},{7,6},{8,9},{9,8},{10,11... | collective-permute-start | bytes 4718600 | tf_op jit(solution)/shard_map/ppermute | solution.py:217
  33.2 45.1 %collective-permute-start.5 = (bf16[512,768]{1,0:T(8,128)(2,1)S(1)}, bf16[512,768]{1,0:T(8,128)(2,1)}, u32[]{:S(2)}, u32[]{:S(2)}) collective-permute-start(bf16[512,768]{1,0:T(8,128)(2,1)S(1)} %get-tuple-element.77), channel_id=1, source_target_pairs={{0,2},{1,3},{2,0},{3,1},{4,6},{5,7},{6,4},{7,5},{8,10},{9,11},{10,... | collective-permute-start | bytes 2359304 | tf_op jit(solution)/shard_map/ppermute | solution.py:217
  35.0 452.4 %reduce-scatter.13.cloned.1.call-start = ((), (), s32[]{:S(2)}) async-start(), calls=%async_computation.10 | async-start | bytes 1290240 | tf_op jit(solution)/shard_map/reduce_scatter | solution.py:234
  79.9 37.2 %collective-permute-start.6 = (bf16[2,512,768]{2,1,0:T(8,128)(2,1)S(1)}, bf16[2,512,768]{2,1,0:T(8,128)(2,1)S(1)}, u32[]{:S(2)}, u32[]{:S(2)}) collective-permute-start(bf16[2,512,768]{2,1,0:T(8,128)(2,1)S(1)} %pad_maximum_fusion.5), channel_id=1, source_target_pairs={{0,1},{1,0},{2,3},{3,2},{4,5},{5,4},{6,7},{7,6},{8,9},{9,8},{10,11... | collective-permute-start | bytes 4718600 | tf_op jit(solution)/shard_map/ppermute | solution.py:217
  115.2 42.9 %collective-permute-start.2 = (bf16[512,192]{1,0:T(8,128)(2,1)S(1)}, bf16[512,192]{1,0:T(8,128)(2,1)S(1)}, u32[]{:S(2)}, u32[]{:S(2)}) collective-permute-start(bf16[512,192]{1,0:T(8,128)(2,1)S(1)} %get-tuple-element.92), channel_id=1, source_target_pairs={{0,1},{1,0},{2,3},{3,2},{4,5},{5,4},{6,7},{7,6},{8,9},{9,8},{10,11... | collective-permute-start | bytes 589832 | tf_op jit(solution)/shard_map/ppermute | solution.py:217
  115.7 46.3 %collective-permute-start.3 = (bf16[512,192]{1,0:T(8,128)(2,1)}, bf16[512,192]{1,0:T(8,128)(2,1)}, u32[]{:S(2)}, u32[]{:S(2)}) collective-permute-start(bf16[512,192]{1,0:T(8,128)(2,1)} %get-tuple-element.91), channel_id=1, source_target_pairs={{0,2},{1,3},{2,0},{3,1},{4,6},{5,7},{6,4},{7,5},{8,10},{9,11},{10,... | collective-permute-start | bytes 589832 | tf_op jit(solution)/shard_map/ppermute | solution.py:217
  116.4 45.7 %collective-permute-start.4 = (bf16[512,192]{1,0:T(8,128)(2,1)S(1)}, bf16[512,192]{1,0:T(8,128)(2,1)}, u32[]{:S(2)}, u32[]{:S(2)}) collective-permute-start(bf16[512,192]{1,0:T(8,128)(2,1)S(1)} %get-tuple-element.90), channel_id=1, source_target_pairs={{0,3},{1,2},{2,1},{3,0},{4,7},{5,6},{6,5},{7,4},{8,11},{9,10},{10,... | collective-permute-start | bytes 589832 | tf_op jit(solution)/shard_map/ppermute | solution.py:217
  157.4 9.5 %collective-permute-start.8 = (bf16[512,192]{1,0:T(8,128)(2,1)}, bf16[512,192]{1,0:T(8,128)(2,1)}, u32[]{:S(2)}, u32[]{:S(2)}) collective-permute-start(bf16[512,192]{1,0:T(8,128)(2,1)} %get-tuple-element.95), channel_id=1, source_target_pairs={{0,2},{1,3},{2,0},{3,1},{4,6},{5,7},{6,4},{7,5},{8,10},{9,11},{10,... | collective-permute-start | bytes 589832 | tf_op jit(solution)/shard_map/ppermute | solution.py:217
  158.8 11.9 %collective-permute-start.9 = (bf16[512,192]{1,0:T(8,128)(2,1)}, bf16[512,192]{1,0:T(8,128)(2,1)}, u32[]{:S(2)}, u32[]{:S(2)}) collective-permute-start(bf16[512,192]{1,0:T(8,128)(2,1)} %get-tuple-element.94), channel_id=1, source_target_pairs={{0,3},{1,2},{2,1},{3,0},{4,7},{5,6},{6,5},{7,4},{8,11},{9,10},{10,... | collective-permute-start | bytes 589832 | tf_op jit(solution)/shard_map/ppermute | solution.py:217
  291.0 9.2 %collective-permute-start.16 = (bf16[512,192]{1,0:T(8,128)(2,1)S(1)}, bf16[512,192]{1,0:T(8,128)(2,1)S(1)}, u32[]{:S(2)}, u32[]{:S(2)}) collective-permute-start(bf16[512,192]{1,0:T(8,128)(2,1)S(1)} %bitcast.153), channel_id=1, source_target_pairs={{0,2},{1,3},{2,0},{3,1},{4,6},{5,7},{6,4},{7,5},{8,10},{9,11},{10,... | collective-permute-start | bytes 589832 | tf_op jit(solution)/shard_map/ppermute | solution.py:217
  292.6 12.4 %collective-permute-start.17 = (bf16[512,192]{1,0:T(8,128)(2,1)S(1)}, bf16[512,192]{1,0:T(8,128)(2,1)S(1)}, u32[]{:S(2)}, u32[]{:S(2)}) collective-permute-start(bf16[512,192]{1,0:T(8,128)(2,1)S(1)} %bitcast.155), channel_id=1, source_target_pairs={{0,3},{1,2},{2,1},{3,0},{4,7},{5,6},{6,5},{7,4},{8,11},{9,10},{10,... | collective-permute-start | bytes 589832 | tf_op jit(solution)/shard_map/ppermute | solution.py:217
  293.1 69.2 %collective-permute-start.10 = (bf16[512,192]{1,0:T(8,128)(2,1)S(1)}, bf16[512,192]{1,0:T(8,128)(2,1)S(1)}, u32[]{:S(2)}, u32[]{:S(2)}) collective-permute-start(bf16[512,192]{1,0:T(8,128)(2,1)S(1)} %bitcast.150), channel_id=1, source_target_pairs={{0,1},{1,0},{2,3},{3,2},{4,5},{5,4},{6,7},{7,6},{8,9},{9,8},{10,11... | collective-permute-start | bytes 589832 | tf_op jit(solution)/shard_map/ppermute | solution.py:217
  293.5 68.8 %collective-permute-start.11 = (bf16[512,192]{1,0:T(8,128)(2,1)S(1)}, bf16[512,192]{1,0:T(8,128)(2,1)S(1)}, u32[]{:S(2)}, u32[]{:S(2)}) collective-permute-start(bf16[512,192]{1,0:T(8,128)(2,1)S(1)} %bitcast.151), channel_id=1, source_target_pairs={{0,2},{1,3},{2,0},{3,1},{4,6},{5,7},{6,4},{7,5},{8,10},{9,11},{10,... | collective-permute-start | bytes 589832 | tf_op jit(solution)/shard_map/ppermute | solution.py:217
  295.1 67.1 %collective-permute-start.12 = (bf16[512,192]{1,0:T(8,128)(2,1)S(1)}, bf16[512,192]{1,0:T(8,128)(2,1)S(1)}, u32[]{:S(2)}, u32[]{:S(2)}) collective-permute-start(bf16[512,192]{1,0:T(8,128)(2,1)S(1)} %bitcast.152), channel_id=1, source_target_pairs={{0,3},{1,2},{2,1},{3,0},{4,7},{5,6},{6,5},{7,4},{8,11},{9,10},{10,... | collective-permute-start | bytes 589832 | tf_op jit(solution)/shard_map/ppermute | solution.py:217
  428.8 156.8 %reduce-scatter.11.cloned.1.call-start = ((), (), s32[]{:S(2)}) async-start(), calls=%async_computation.9 | async-start | bytes 5308416 | tf_op jit(solution)/shard_map/reduce_scatter | solution.py:234
  438.8 214.6 %reduce-scatter.7.cloned.1.call-start = ((), (), s32[]{:S(2)}) async-start(), calls=%async_computation.7 | async-start | bytes 1548288 | tf_op jit(solution)/shard_map/reduce_scatter | solution.py:234
  446.6 304.7 %reduce-scatter.9.cloned.1.call-start = ((), (), s32[]{:S(2)}) async-start(), calls=%async_computation.8 | async-start | bytes 5308416 | tf_op jit(solution)/shard_map/reduce_scatter | solution.py:234
  463.1 7.7 collective-permute-start.18
  472.7 40.5 %collective-permute-start.19 = (bf16[512,768]{1,0:T(8,128)(2,1)}, bf16[512,768]{1,0:T(8,128)(2,1)}, u32[]{:S(2)}, u32[]{:S(2)}) collective-permute-start(bf16[512,768]{1,0:T(8,128)(2,1)} %fusion.12), channel_id=1, source_target_pairs={{0,2},{1,3},{2,0},{3,1},{4,6},{5,7},{6,4},{7,5},{8,10},{9,11},{10,... | collective-permute-start | bytes 2359304 | tf_op jit(solution)/shard_map/ppermute | solution.py:217
  478.6 34.7 %collective-permute-start.14 = (bf16[512,768]{1,0:T(8,128)(2,1)}, bf16[512,768]{1,0:T(8,128)(2,1)}, u32[]{:S(2)}, u32[]{:S(2)}) collective-permute-start(bf16[512,768]{1,0:T(8,128)(2,1)} %fusion.17), channel_id=1, source_target_pairs={{0,2},{1,3},{2,0},{3,1},{4,6},{5,7},{6,4},{7,5},{8,10},{9,11},{10,... | collective-permute-start | bytes 2359304 | tf_op jit(solution)/shard_map/ppermute | solution.py:217
  487.4 24.9 %collective-permute-start.20 = (bf16[112,576]{1,0:T(8,128)(2,1)}, bf16[112,576]{1,0:T(8,128)(2,1)S(1)}, u32[]{:S(2)}, u32[]{:S(2)}) collective-permute-start(bf16[112,576]{1,0:T(8,128)(2,1)} %reduce-scatter.13.cloned.1.call-done), channel_id=1, source_target_pairs={{0,2},{1,3},{2,0},{3,1},{4,6},{5,7},{6,4},{7,5},{8,10},{9,11},{10,... | collective-permute-start | bytes 387080 | tf_op jit(solution)/shard_map/ppermute | solution.py:217
  513.2 6.0 collective-permute-start.21
  585.6 171.9 %collective-permute-start.26 = (bf16[384,768]{1,0:T(8,128)(2,1)}, bf16[384,768]{1,0:T(8,128)(2,1)}, u32[]{:S(2)}, u32[]{:S(2)}) collective-permute-start(bf16[384,768]{1,0:T(8,128)(2,1)} %reduce-scatter.11.cloned.1.call-done), channel_id=1, source_target_pairs={{0,1},{1,0},{2,3},{3,2},{4,5},{5,4},{6,7},{7,6},{8,9},{9,8},{10,11... | collective-permute-start | bytes 1769480 | tf_op jit(solution)/shard_map/ppermute | solution.py:217
  653.4 101.5 %collective-permute-start.22 = (bf16[112,768]{1,0:T(8,128)(2,1)}, bf16[112,768]{1,0:T(8,128)(2,1)}, u32[]{:S(2)}, u32[]{:S(2)}) collective-permute-start(bf16[112,768]{1,0:T(8,128)(2,1)} %reduce-scatter.7.cloned.1.call-done), channel_id=1, source_target_pairs={{0,1},{1,0},{2,3},{3,2},{4,5},{5,4},{6,7},{7,6},{8,9},{9,8},{10,11... | collective-permute-start | bytes 516104 | tf_op jit(solution)/shard_map/ppermute | solution.py:217
  751.3 8.0 %collective-permute-start.24 = (bf16[96,3072]{1,0:T(8,128)(2,1)}, bf16[96,3072]{1,0:T(8,128)(2,1)}, u32[]{:S(2)}, u32[]{:S(2)}) collective-permute-start(bf16[96,3072]{1,0:T(8,128)(2,1)} %reduce-scatter.9.cloned.1.call-done), channel_id=1, source_target_pairs={{0,1},{1,0},{2,3},{3,2},{4,5},{5,4},{6,7},{7,6},{8,9},{9,8},{10,11... | collective-permute-start | bytes 1769480 | tf_op jit(solution)/shard_map/ppermute | solution.py:217
  755.9 7.2 collective-permute-start.23
  758.6 17.1 %collective-permute-start.27 = (bf16[384,768]{1,0:T(8,128)(2,1)S(1)}, bf16[384,768]{1,0:T(8,128)(2,1)S(1)}, u32[]{:S(2)}, u32[]{:S(2)}) collective-permute-start(bf16[384,768]{1,0:T(8,128)(2,1)S(1)} %add_convert_fusion.4), channel_id=1, source_target_pairs={{0,2},{1,3},{2,0},{3,1},{4,6},{5,7},{6,4},{7,5},{8,10},{9,11},{10,... | collective-permute-start | bytes 1769480 | tf_op jit(solution)/shard_map/ppermute | solution.py:217
  760.5 27.5 %collective-permute-start.25 = (bf16[96,3072]{1,0:T(8,128)(2,1)S(1)}, bf16[96,3072]{1,0:T(8,128)(2,1)S(1)}, u32[]{:S(2)}, u32[]{:S(2)}) collective-permute-start(bf16[96,3072]{1,0:T(8,128)(2,1)S(1)} %add_convert_fusion.5), channel_id=1, source_target_pairs={{0,2},{1,3},{2,0},{3,1},{4,6},{5,7},{6,4},{7,5},{8,10},{9,11},{10,... | collective-permute-start | bytes 1769480 | tf_op jit(solution)/shard_map/ppermute | solution.py:217
  (76 other events, 1189.5 us)
Sparse Core Ops, SparseCore 0:
  10.2 53.3 all-gather.4
  65.8 82.2 all-gather.6
  150.3 78.0 all-gather.8
  428.9 58.3 reduce-scatter.12
  490.8 94.6 reduce-scatter.10
  588.8 64.4 reduce-scatter.6
  657.0 94.2 reduce-scatter.8

commit v2 on v1

--- a/solution.py
+++ b/solution.py
@@ -325,11 +325,11 @@
     grad_second, grad_g_two, grad_s_two = second_back(grad_result)
     grad_branch = grad_second.astype(bf16)
     grad_down_bias = jnp.sum(grad_branch.astype(f32), axis=0)
-    sh_down = scatter_sum(inner_rows(active_low, grad_branch))
+    grad_down = inner_rows(active_low, grad_branch).astype(bf16)
     (grad_inner,) = gelu_back(inner_cols(grad_branch, w_down))
     grad_pre = grad_inner.astype(bf16)
     grad_up_bias = jnp.sum(grad_pre.astype(f32), axis=0)
-    sh_up = scatter_sum(inner_rows(first_low, grad_pre))
+    grad_up = inner_rows(first_low, grad_pre).astype(bf16)
     grad_first = grad_second + inner_cols(grad_pre, w_up)
     grad_mid, grad_g_one, grad_s_one = first_back(grad_first)
     grad_attended = grad_mid.astype(bf16)
@@ -344,7 +344,13 @@
     out_all = jnp.concatenate(
         [grad_out.astype(bf16).reshape(parts, shard, width), rest_all.reshape(parts, rest_rows, width)], axis=1
     )
-    sh_out = scatter_sum(out_all.reshape(parts * (shard + rest_rows), width))
+    out_all = out_all.reshape(parts * (shard + rest_rows), width)
+    grad_down, grad_up, out_all, grad_ctx = lax.optimization_barrier(
+        (grad_down, grad_up, out_all, grad_ctx)
+    )
+    sh_down = scatter_sum(grad_down)
+    sh_up = scatter_sum(grad_up)
+    sh_out = scatter_sum(out_all)
 
     grad_qkv = jnp.zeros((width, wide), f32)
     bias_sums = jnp.zeros((wide,), f32)
@@ -373,6 +379,7 @@
     qkv_all = jnp.concatenate(
         [grad_qkv.reshape(parts, shard, wide), bias_full.reshape(parts, bias_rows, wide)], axis=1
     )
+    qkv_all, sh_down, sh_up, sh_out = lax.optimization_barrier((qkv_all, sh_down, sh_up, sh_out))
     sh_qkv = scatter_sum(qkv_all.reshape(parts * (shard + bias_rows), wide))
     far = swap(sh_qkv, 2)
     both = jnp.stack([sh_qkv, far])

time: 800 us -> 659 us (0.82)
  waiting for transfers between devices: 336 us -> 198 us
    reduce_scatter x4, waiting for transfers between devices: 239 us -> 135 us  [scatter_sum(): lax.psum_scatter(values.astype(jnp.bfloat16), 'dp', scatter_dimension=0,...]
    ppermute x28, waiting for transfers between devices: 82.2 us -> 44.3 us  [swap(): return lax.ppermute(values, 'seq', pairs)]
  transfers between devices with their start and end apart: 35 -> 35, of which waited for: 14 -> 11; matrix products, arithmetic and copies ran while one was open for 17% -> 20% of each run, Pallas kernels for 14% -> 25%
where the time goes in v2:
time: 659 us; the launch traced here: 655 us
  waiting for transfers between devices  198 us (30%)
  Pallas kernels  161 us (24%)
  matrix products  128 us (19%)
  other arithmetic  56.4 us (9%)
  local copies, waits for them, and re-layouts  38 us (6%)
  blocking collectives  36.2 us (5%)
  starting transfers between devices  21.6 us (3%)
  between operations  15.5 us (2%)
    reduce_scatter x4, waiting for transfers between devices, scatter_sum(): lax.psum_scatter(values.astype(jnp.bfloat16), 'dp', scatter_dimension=0,...  135 us
    pallas_call x2, Pallas kernels, attend_backward(): pl.pallas_call(functools.partial(bwd_kernel, heads, local_len), grid_spec...  97.8 us
    pallas_call x2, Pallas kernels, attend_forward(): pl.pallas_call(functools.partial(fwd_kernel, heads, local_len), grid_spec...  56.1 us
    dot_general x3, matrix products, matmul(): return jnp.dot(first_op, second_op, preferred_element_type=jnp.float32)  52.5 us
    dot_general x5, matrix products, inner_cols(): lax.dot_general(first_op, second_op, (((1,), (1,)), ((), ())), preferred_...  47.1 us
    ppermute x28, waiting for transfers between devices, swap(): return lax.ppermute(values, 'seq', pairs)  44.3 us
    all_gather x1, blocking collectives, shards(): lax.all_gather(jnp.concatenate([qkv_own, small]), 'dp', axis=0, tiled=False)  36.2 us
    dot_general x5, matrix products, inner_rows(): lax.dot_general(first_op, second_op, (((0,), (0,)), ((), ())), preferred_...  28.4 us
  transfers between devices with their start and end apart: 35, of which 11 were waited for; matrix products, arithmetic and copies ran while one was open for 20% of the time, Pallas kernels for 25%

profile of v2, /device:TPU:0, one launch (start us, length us, event | category | flops | bytes accessed | tf_op | source)
XLA Modules:
  0.0 655.2 jit_solution(17155474208262047624)
XLA Ops:
  14.2 17.5 %collective-permute-done.5 = bf16[512,768]{1,0:T(8,128)(2,1)S(1)} collective-permute-done((bf16[512,768]{1,0:T(8,128)(2,1)S(1)}, bf16[512,768]{1,0:T(8,128)(2,1)S(1)}, u32[]{:S(2)}, u32[]{:S(2)}) %collective-permute-start.5) | collective-permute-done | bytes 786464 | tf_op jit(solution)/shard_map/ppermute | solution.py:217
  37.7 36.2 %all-gather = bf16[896,576]{1,0:T(8,128)(2,1)S(1)} all-gather(bf16[112,576]{1,0:T(8,128)(2,1)S(1)} %copy.67), channel_id=2, replica_groups=mesh['dp'=8,'seq'=4] {'dp'}, dimensions={0}, use_global_device_ids=true | all-gather | bytes 1161216 | tf_op jit(solution)/shard_map/all_gather | solution.py:273
  82.1 3.7 project.3
  85.8 28.0 %attend_forward.3 = (bf16[2048,192]{1,0:T(8,128)(2,1)S(1)}, f32[3,1,2048]{2,1,0:T(1,128)S(1)}) custom-call(s32[2]{0:T(128)S(1)} %get-tuple-element.152.meta_ref, bf16[3,2048,64]{2,1,0:T(8,128)(2,1)S(1)} %get-tuple-element.43.q_ref, bf16[3,2048,64]{2,1,0:T(8,128)(2,1)S(1)} %get-tuple-element.44.k_ref, bf16[3,2048,64]{2,1,0:T(8,128)(2,1)S(1)} %get-tuple-element.45.v_ref), custom_call_target="tpu_custom_call" | custom-call | flops 12884901888 | bytes 3145728 | tf_op jit(solution)/shard_map/attend_forward/pallas_call | solution.py:81
  118.2 3.7 project.2
  122.0 28.1 %attend_forward.2 = (bf16[2048,192]{1,0:T(8,128)(2,1)S(1)}, f32[3,1,2048]{2,1,0:T(1,128)S(1)}) custom-call(s32[2]{0:T(128)S(1)} %get-tuple-element.151.meta_ref, bf16[3,2048,64]{2,1,0:T(8,128)(2,1)S(1)} %get-tuple-element.39.q_ref, bf16[3,2048,64]{2,1,0:T(8,128)(2,1)S(1)} %get-tuple-element.40.k_ref, bf16[3,2048,64]{2,1,0:T(8,128)(2,1)S(1)} %get-tuple-element.41.v_ref), custom_call_target="tpu_custom_call" | custom-call | flops 12884901888 | bytes 3145728 | tf_op jit(solution)/shard_map/attend_forward/pallas_call | solution.py:81
  159.2 6.3 collective-permute-done.3
  165.5 5.1 fusion.47
  173.6 38.1 %multiply_convert_fusion = (bf16[1024,3072]{1,0:T(8,128)(2,1)}, f32[1024,3072]{1,0:T(8,128)}, f32[1024,3072]{1,0:T(8,128)}) fusion(f32[3072]{0:T(1024)S(1)} %reshape.295, bf16[768,3072]{1,0:T(8,128)(2,1)} %all-gather.7.cloned.1.call-done, f32[1024,768]{1,0:T(8,128)} %get-tuple-element.140, f32[768]{0:T(1024)S(1)} %reshape.294, f32[768]{0:T(1024)S(1)} %reshape.293, ...), kind=kOutput, calls=%fused_computation.3 | convolution fusion | flops 5043388416 | bytes 39348224 | tf_op jit(solution)/shard_map/dot_general | solution.py:27
  211.8 16.9 %all-gather.9.cloned.1.call-done = bf16[3072,768]{1,0:T(8,128)(2,1)} async-done(((bf16[384,768]{1,0:T(8,128)(2,1)}), bf16[3072,768]{1,0:T(8,128)(2,1)}) %all-gather.9.cloned.1.call-update) | async-done | bytes 4718608 | tf_op jit(solution)/shard_map/all_gather | solution.py:285
  228.6 9.3 %fusion.48 = (f32[1024]{0:T(1024)S(1)}, f32[1024,768]{1,0:T(8,128)S(1)}) fusion(f32[768]{0:T(1024)S(1)} %reshape.296, bf16[1024,3072]{1,0:T(8,128)(2,1)} %get-tuple-element.76, bf16[3072,768]{1,0:T(8,128)(2,1)} %all-gather.9.cloned.1.call-done, f32[768]{0:T(1024)S(1)} %reshape.294, f32[768]{0:T(1024)S(1)} %reshape.293, f32[1024]{0:T(1024)S(1)} %fusion.23, ...), kind=kOutput, calls=%fused_computation.159 | convolution fusion | flops 4837342208 | bytes 17323008 | tf_op jit(solution)/shard_map/dot_general | solution.py:27
  239.8 3.5 fusion.38
  245.6 7.0 %convolution_convert_fusion.1 = bf16[3072,768]{1,0:T(8,128)(2,1)} fusion(bf16[1024,3072]{1,0:T(8,128)(2,1)S(1)} %bitcast.147, bf16[1024,768]{1,0:T(8,128)(2,1)S(1)} %get-tuple-element.69), kind=kOutput, calls=%fused_computation.20 | convolution fusion | flops 4834197504 | bytes 12582912 | tf_op jit(solution)/shard_map/dot_general | solution.py:31
  252.6 16.7 %fusion.49 = (bf16[3072]{0:T(1024)(128)(2,1)S(1)}, bf16[1024,3072]{1,0:T(8,128)(2,1)}) fusion(f32[1024,3072]{1,0:T(8,128)} %get-tuple-element.77, bf16[1024,768]{1,0:T(8,128)(2,1)S(1)} %get-tuple-element.69, bf16[3072,768]{1,0:T(8,128)(2,1)} %all-gather.9.cloned.1.call-done, f32[1024,3072]{1,0:T(8,128)} %get-tuple-element.141, f32[3072]{0:T(1024)S(1)} %reshape.295), kind=kOutput, calls=%fused_computation.160 | convolution fusion | flops 4882166784 | bytes 37767168 | tf_op jit(solution)/shard_map/dot_general | solution.py:37
  269.3 10.4 %convolution_convert_fusion = bf16[768,3072]{1,0:T(8,128)(2,1)} fusion(bf16[1024,3072]{1,0:T(8,128)(2,1)} %get-tuple-element.146, f32[1024,768]{1,0:T(8,128)} %get-tuple-element.140, f32[768]{0:T(1024)S(1)} %reshape.294, f32[768]{0:T(1024)S(1)} %reshape.293, f32[1024]{0:T(1024)S(1)} %fusion.23, f32[1024]{0:T(1024)S(1)} %broadcast_multiply_fusion.1), kind=kOutput, calls=%fused_computation.19 | convolution fusion | flops 4838129664 | bytes 14170112 | tf_op jit(solution)/shard_map/dot_general | solution.py:31
  279.7 11.2 %multiply_reduce_fusion = (bf16[768]{0:T(1024)(128)(2,1)S(1)}, f32[1024]{0:T(1024)S(1)}, bf16[768]{0:T(1024)(128)(2,1)S(1)}, f32[1024,768]{1,0:T(8,128)S(1)}) fusion(f32[1024,768]{1,0:T(8,128)} %get-tuple-element.140, f32[1024]{0:T(1024)S(1)} %fusion.23, f32[1024]{0:T(1024)S(1)} %broadcast_multiply_fusion.1, f32[768]{0:T(1024)S(1)} %reshape.293, ...), kind=kOutput, calls=%fused_computation.32 | convolution fusion | flops 4839699456 | bytes 20469760 | tf_op jit(solution)/shard_map/dot_general | solution.py:37
  297.2 4.7 convolution_convert_fusion.2
  313.6 4.6 copy.72
  323.2 5.0 collective-permute-done.12
  328.3 5.6 collective-permute-done.11
  335.0 48.7 %attend_backward.2 = (bf16[2048,192]{1,0:T(8,128)(2,1)}, bf16[2048,192]{1,0:T(8,128)(2,1)}, bf16[2048,192]{1,0:T(8,128)(2,1)}) custom-call(s32[2]{0:T(128)} %copy-done.3, bf16[3,2048,64]{2,1,0:T(8,128)(2,1)} %copy-done.7, bf16[3,2048,64]{2,1,0:T(8,128)(2,1)} %copy-done.8, bf16[3,2048,64]{2,1,0:T(8,128)(2,1)} %copy-done.9, ...), custom_call_target="tpu_custom_call" | custom-call | flops 32212254720 | bytes 6291456 | tf_op jit(solution)/shard_map/attend_backward/pallas_call | solution.py:159
  383.8 7.2 %fusion.50 = (bf16[2048,768]{1,0:T(8,128)(2,1)S(1)}, f32[2048,768]{1,0:T(8,128)}) fusion(bf16[768,576]{1,0:T(8,128)(2,1)S(1)} %bitcast.121, bf16[2048,192]{1,0:T(8,128)(2,1)} %get-tuple-element.51, bf16[2048,192]{1,0:T(8,128)(2,1)} %get-tuple-element.50, bf16[2048,192]{1,0:T(8,128)(2,1)} %get-tuple-element.49), kind=kOutput, calls=%fused_computation.161 | convolution fusion | flops 1820590080 | bytes 12681216 | tf_op jit(solution)/shard_map/dot_general | solution.py:37
  393.5 49.1 %attend_backward.3 = (bf16[2048,192]{1,0:T(8,128)(2,1)}, bf16[2048,192]{1,0:T(8,128)(2,1)}, bf16[2048,192]{1,0:T(8,128)(2,1)}) custom-call(s32[2]{0:T(128)} %copy-done.2, bf16[3,2048,64]{2,1,0:T(8,128)(2,1)} %copy-done.4, bf16[3,2048,64]{2,1,0:T(8,128)(2,1)} %copy-done.5, bf16[3,2048,64]{2,1,0:T(8,128)(2,1)} %copy-done.6, ...), custom_call_target="tpu_custom_call" | custom-call | flops 32212254720 | bytes 6291456 | tf_op jit(solution)/shard_map/attend_backward/pallas_call | solution.py:159
  442.6 7.3 %fusion.51 = (bf16[2048,768]{1,0:T(8,128)(2,1)S(1)}, f32[2048,768]{1,0:T(8,128)}) fusion(bf16[768,576]{1,0:T(8,128)(2,1)S(1)} %bitcast.122, bf16[2048,192]{1,0:T(8,128)(2,1)} %get-tuple-element.55, bf16[2048,192]{1,0:T(8,128)(2,1)} %get-tuple-element.54, bf16[2048,192]{1,0:T(8,128)(2,1)} %get-tuple-element.53), kind=kOutput, calls=%fused_computation.162 | convolution fusion | flops 1820590080 | bytes 12681216 | tf_op jit(solution)/shard_map/dot_general | solution.py:37
  458.2 4.4 fusion.30
  468.2 3.4 convert_element_type.274
  471.6 3.1 fusion.12
  475.4 3.6 convolution_add_fusion
  483.6 89.0 %reduce-scatter.9.cloned.1.call-done = bf16[96,3072]{1,0:T(8,128)(2,1)} async-done(((bf16[768,3072]{1,0:T(8,128)(2,1)}), bf16[96,3072]{1,0:T(8,128)(2,1)}) %reduce-scatter.9.cloned.1.call-update) | async-done | bytes 589840 | tf_op jit(solution)/shard_map/reduce_scatter | solution.py:234
  573.2 4.5 fusion.21
  581.5 4.9 collective-permute-done.23
  590.1 46.1 %reduce-scatter.13.cloned.1.call-done = bf16[112,576]{1,0:T(8,128)(2,1)} async-done(((bf16[896,576]{1,0:T(8,128)(2,1)}), bf16[112,576]{1,0:T(8,128)(2,1)}) %reduce-scatter.13.cloned.1.call-update) | async-done | bytes 129040 | tf_op jit(solution)/shard_map/reduce_scatter | solution.py:234
  (311 shorter events, 106.7 us)
Async XLA Ops:
  7.2 148.7 %all-gather.5.cloned.1.call-start = ((), (), s32[]{:S(2)}) async-start(), calls=%async_computation.4 | async-start | bytes 1327104 | tf_op jit(solution)/shard_map/all_gather | solution.py:283
  7.9 165.7 %all-gather.7.cloned.1.call-start = ((), (), s32[]{:S(2)}) async-start(), calls=%async_computation.5 | async-start | bytes 5308416 | tf_op jit(solution)/shard_map/all_gather | solution.py:284
  8.8 219.9 %all-gather.9.cloned.1.call-start = ((), (), s32[]{:S(2)}) async-start(), calls=%async_computation.6 | async-start | bytes 5308416 | tf_op jit(solution)/shard_map/all_gather | solution.py:285
  11.3 20.5 %collective-permute-start.5 = (bf16[512,768]{1,0:T(8,128)(2,1)S(1)}, bf16[512,768]{1,0:T(8,128)(2,1)S(1)}, u32[]{:S(2)}, u32[]{:S(2)}) collective-permute-start(bf16[512,768]{1,0:T(8,128)(2,1)S(1)} %get-tuple-element.93), channel_id=1, source_target_pairs={{0,2},{1,3},{2,0},{3,1},{4,6},{5,7},{6,4},{7,5},{8,10},{9,11},{10,... | collective-permute-start | bytes 2359304 | tf_op jit(solution)/shard_map/ppermute | solution.py:217
  33.2 46.6 %collective-permute-start.6 = (bf16[2,512,768]{2,1,0:T(8,128)(2,1)}, bf16[2,512,768]{2,1,0:T(8,128)(2,1)}, u32[]{:S(2)}, u32[]{:S(2)}) collective-permute-start(bf16[2,512,768]{2,1,0:T(8,128)(2,1)} %pad_maximum_fusion.6), channel_id=1, source_target_pairs={{0,1},{1,0},{2,3},{3,2},{4,5},{5,4},{6,7},{7,6},{8,9},{9,8},{10,11... | collective-permute-start | bytes 4718600 | tf_op jit(solution)/shard_map/ppermute | solution.py:217
  33.2 44.9 %collective-permute-start = (bf16[512,768]{1,0:T(8,128)(2,1)S(1)}, bf16[512,768]{1,0:T(8,128)(2,1)S(1)}, u32[]{:S(2)}, u32[]{:S(2)}) collective-permute-start(bf16[512,768]{1,0:T(8,128)(2,1)S(1)} %get-tuple-element.92), channel_id=1, source_target_pairs={{0,2},{1,3},{2,0},{3,1},{4,6},{5,7},{6,4},{7,5},{8,10},{9,11},{10,... | collective-permute-start | bytes 2359304 | tf_op jit(solution)/shard_map/ppermute | solution.py:217
  34.9 448.6 %reduce-scatter.11.cloned.1.call-start = ((), (), s32[]{:S(2)}) async-start(), calls=%async_computation.9 | async-start | bytes 1548288 | tf_op jit(solution)/shard_map/reduce_scatter | solution.py:234
  79.7 37.3 %collective-permute-start.1 = (bf16[2,512,768]{2,1,0:T(8,128)(2,1)S(1)}, bf16[2,512,768]{2,1,0:T(8,128)(2,1)S(1)}, u32[]{:S(2)}, u32[]{:S(2)}) collective-permute-start(bf16[2,512,768]{2,1,0:T(8,128)(2,1)S(1)} %pad_maximum_fusion.5), channel_id=1, source_target_pairs={{0,1},{1,0},{2,3},{3,2},{4,5},{5,4},{6,7},{7,6},{8,9},{9,8},{10,11... | collective-permute-start | bytes 4718600 | tf_op jit(solution)/shard_map/ppermute | solution.py:217
  114.9 38.2 %collective-permute-start.9 = (bf16[512,192]{1,0:T(8,128)(2,1)S(1)}, bf16[512,192]{1,0:T(8,128)(2,1)S(1)}, u32[]{:S(2)}, u32[]{:S(2)}) collective-permute-start(bf16[512,192]{1,0:T(8,128)(2,1)S(1)} %get-tuple-element.110), channel_id=1, source_target_pairs={{0,3},{1,2},{2,1},{3,0},{4,7},{5,6},{6,5},{7,4},{8,11},{9,10},{10,... | collective-permute-start | bytes 589832 | tf_op jit(solution)/shard_map/ppermute | solution.py:217
  116.1 41.3 %collective-permute-start.8 = (bf16[512,192]{1,0:T(8,128)(2,1)}, bf16[512,192]{1,0:T(8,128)(2,1)}, u32[]{:S(2)}, u32[]{:S(2)}) collective-permute-start(bf16[512,192]{1,0:T(8,128)(2,1)} %get-tuple-element.111), channel_id=1, source_target_pairs={{0,2},{1,3},{2,0},{3,1},{4,6},{5,7},{6,4},{7,5},{8,10},{9,11},{10,... | collective-permute-start | bytes 589832 | tf_op jit(solution)/shard_map/ppermute | solution.py:217
  117.0 40.4 %collective-permute-start.7 = (bf16[512,192]{1,0:T(8,128)(2,1)}, bf16[512,192]{1,0:T(8,128)(2,1)}, u32[]{:S(2)}, u32[]{:S(2)}) collective-permute-start(bf16[512,192]{1,0:T(8,128)(2,1)} %get-tuple-element.112), channel_id=1, source_target_pairs={{0,1},{1,0},{2,3},{3,2},{4,5},{5,4},{6,7},{7,6},{8,9},{9,8},{10,11... | collective-permute-start | bytes 589832 | tf_op jit(solution)/shard_map/ppermute | solution.py:217
  151.0 8.3 %collective-permute-start.4 = (bf16[512,192]{1,0:T(8,128)(2,1)}, bf16[512,192]{1,0:T(8,128)(2,1)}, u32[]{:S(2)}, u32[]{:S(2)}) collective-permute-start(bf16[512,192]{1,0:T(8,128)(2,1)} %get-tuple-element.106), channel_id=1, source_target_pairs={{0,3},{1,2},{2,1},{3,0},{4,7},{5,6},{6,5},{7,4},{8,11},{9,10},{10,... | collective-permute-start | bytes 589832 | tf_op jit(solution)/shard_map/ppermute | solution.py:217
  152.2 13.3 %collective-permute-start.3 = (bf16[512,192]{1,0:T(8,128)(2,1)}, bf16[512,192]{1,0:T(8,128)(2,1)}, u32[]{:S(2)}, u32[]{:S(2)}) collective-permute-start(bf16[512,192]{1,0:T(8,128)(2,1)} %get-tuple-element.107), channel_id=1, source_target_pairs={{0,2},{1,3},{2,0},{3,1},{4,6},{5,7},{6,4},{7,5},{8,10},{9,11},{10,... | collective-permute-start | bytes 589832 | tf_op jit(solution)/shard_map/ppermute | solution.py:217
  153.1 12.4 %collective-permute-start.2 = (bf16[512,192]{1,0:T(8,128)(2,1)S(1)}, bf16[512,192]{1,0:T(8,128)(2,1)}, u32[]{:S(2)}, u32[]{:S(2)}) collective-permute-start(bf16[512,192]{1,0:T(8,128)(2,1)S(1)} %get-tuple-element.108), channel_id=1, source_target_pairs={{0,1},{1,0},{2,3},{3,2},{4,5},{5,4},{6,7},{7,6},{8,9},{9,8},{10,11... | collective-permute-start | bytes 589832 | tf_op jit(solution)/shard_map/ppermute | solution.py:217
  312.9 170.6 %reduce-scatter.7.cloned.1.call-start = ((), (), s32[]{:S(2)}) async-start(), calls=%async_computation.7 | async-start | bytes 5308416 | tf_op jit(solution)/shard_map/reduce_scatter | solution.py:234
  313.5 259.0 %reduce-scatter.9.cloned.1.call-start = ((), (), s32[]{:S(2)}) async-start(), calls=%async_computation.8 | async-start | bytes 5308416 | tf_op jit(solution)/shard_map/reduce_scatter | solution.py:234
  319.4 8.8 %collective-permute-start.12 = (bf16[512,192]{1,0:T(8,128)(2,1)}, bf16[512,192]{1,0:T(8,128)(2,1)S(1)}, u32[]{:S(2)}, u32[]{:S(2)}) collective-permute-start(bf16[512,192]{1,0:T(8,128)(2,1)} %get-tuple-element.86), channel_id=1, source_target_pairs={{0,3},{1,2},{2,1},{3,0},{4,7},{5,6},{6,5},{7,4},{8,11},{9,10},{10,... | collective-permute-start | bytes 589832 | tf_op jit(solution)/shard_map/ppermute | solution.py:217
  319.4 14.5 %collective-permute-start.11 = (bf16[512,192]{1,0:T(8,128)(2,1)}, bf16[512,192]{1,0:T(8,128)(2,1)S(1)}, u32[]{:S(2)}, u32[]{:S(2)}) collective-permute-start(bf16[512,192]{1,0:T(8,128)(2,1)} %get-tuple-element.87), channel_id=1, source_target_pairs={{0,2},{1,3},{2,0},{3,1},{4,6},{5,7},{6,4},{7,5},{8,10},{9,11},{10,... | collective-permute-start | bytes 589832 | tf_op jit(solution)/shard_map/ppermute | solution.py:217
  321.0 12.9 %collective-permute-start.10 = (bf16[512,192]{1,0:T(8,128)(2,1)}, bf16[512,192]{1,0:T(8,128)(2,1)S(1)}, u32[]{:S(2)}, u32[]{:S(2)}) collective-permute-start(bf16[512,192]{1,0:T(8,128)(2,1)} %get-tuple-element.88), channel_id=1, source_target_pairs={{0,1},{1,0},{2,3},{3,2},{4,5},{5,4},{6,7},{7,6},{8,9},{9,8},{10,11... | collective-permute-start | bytes 589832 | tf_op jit(solution)/shard_map/ppermute | solution.py:217
  321.3 71.0 %collective-permute-start.17 = (bf16[512,192]{1,0:T(8,128)(2,1)}, bf16[512,192]{1,0:T(8,128)(2,1)S(1)}, u32[]{:S(2)}, u32[]{:S(2)}) collective-permute-start(bf16[512,192]{1,0:T(8,128)(2,1)} %get-tuple-element.82), channel_id=1, source_target_pairs={{0,3},{1,2},{2,1},{3,0},{4,7},{5,6},{6,5},{7,4},{8,11},{9,10},{10,... | collective-permute-start | bytes 589832 | tf_op jit(solution)/shard_map/ppermute | solution.py:217
  322.4 69.9 %collective-permute-start.16 = (bf16[512,192]{1,0:T(8,128)(2,1)}, bf16[512,192]{1,0:T(8,128)(2,1)S(1)}, u32[]{:S(2)}, u32[]{:S(2)}) collective-permute-start(bf16[512,192]{1,0:T(8,128)(2,1)} %get-tuple-element.83), channel_id=1, source_target_pairs={{0,2},{1,3},{2,0},{3,1},{4,6},{5,7},{6,4},{7,5},{8,10},{9,11},{10,... | collective-permute-start | bytes 589832 | tf_op jit(solution)/shard_map/ppermute | solution.py:217
  323.2 313.1 %reduce-scatter.13.cloned.1.call-start = ((), (), s32[]{:S(2)}) async-start(), calls=%async_computation.10 | async-start | bytes 1290240 | tf_op jit(solution)/shard_map/reduce_scatter | solution.py:234
  328.2 64.1 %collective-permute-start.15 = (bf16[512,192]{1,0:T(8,128)(2,1)S(1)}, bf16[512,192]{1,0:T(8,128)(2,1)S(1)}, u32[]{:S(2)}, u32[]{:S(2)}) collective-permute-start(bf16[512,192]{1,0:T(8,128)(2,1)S(1)} %copy-done.39), channel_id=1, source_target_pairs={{0,1},{1,0},{2,3},{3,2},{4,5},{5,4},{6,7},{7,6},{8,9},{9,8},{10,11... | collective-permute-start | bytes 589832 | tf_op jit(solution)/shard_map/ppermute | solution.py:217
  392.2 70.4 %collective-permute-start.13 = (bf16[2,512,768]{2,1,0:T(8,128)(2,1)}, bf16[2,512,768]{2,1,0:T(8,128)(2,1)}, u32[]{:S(2)}, u32[]{:S(2)}) collective-permute-start(bf16[2,512,768]{2,1,0:T(8,128)(2,1)} %slice.231), channel_id=1, source_target_pairs={{0,1},{1,0},{2,3},{3,2},{4,5},{5,4},{6,7},{7,6},{8,9},{9,8},{10,11... | collective-permute-start | bytes 4718600 | tf_op jit(solution)/shard_map/ppermute | solution.py:217
  451.1 17.0 %collective-permute-start.18 = (bf16[2,512,768]{2,1,0:T(8,128)(2,1)}, bf16[2,512,768]{2,1,0:T(8,128)(2,1)}, u32[]{:S(2)}, u32[]{:S(2)}) collective-permute-start(bf16[2,512,768]{2,1,0:T(8,128)(2,1)} %slice.241), channel_id=1, source_target_pairs={{0,1},{1,0},{2,3},{3,2},{4,5},{5,4},{6,7},{7,6},{8,9},{9,8},{10,11... | collective-permute-start | bytes 4718600 | tf_op jit(solution)/shard_map/ppermute | solution.py:217
  466.8 106.4 %collective-permute-start.14 = (bf16[512,768]{1,0:T(8,128)(2,1)}, bf16[512,768]{1,0:T(8,128)(2,1)}, u32[]{:S(2)}, u32[]{:S(2)}) collective-permute-start(bf16[512,768]{1,0:T(8,128)(2,1)} %fusion.17), channel_id=1, source_target_pairs={{0,2},{1,3},{2,0},{3,1},{4,6},{5,7},{6,4},{7,5},{8,10},{9,11},{10,... | collective-permute-start | bytes 2359304 | tf_op jit(solution)/shard_map/ppermute | solution.py:217
  474.7 98.4 %collective-permute-start.19 = (bf16[512,768]{1,0:T(8,128)(2,1)}, bf16[512,768]{1,0:T(8,128)(2,1)}, u32[]{:S(2)}, u32[]{:S(2)}) collective-permute-start(bf16[512,768]{1,0:T(8,128)(2,1)} %fusion.12), channel_id=1, source_target_pairs={{0,2},{1,3},{2,0},{3,1},{4,6},{5,7},{6,4},{7,5},{8,10},{9,11},{10,... | collective-permute-start | bytes 2359304 | tf_op jit(solution)/shard_map/ppermute | solution.py:217
  572.7 8.0 %collective-permute-start.24 = (bf16[96,3072]{1,0:T(8,128)(2,1)}, bf16[96,3072]{1,0:T(8,128)(2,1)S(1)}, u32[]{:S(2)}, u32[]{:S(2)}) collective-permute-start(bf16[96,3072]{1,0:T(8,128)(2,1)} %reduce-scatter.9.cloned.1.call-done), channel_id=1, source_target_pairs={{0,1},{1,0},{2,3},{3,2},{4,5},{5,4},{6,7},{7,6},{8,9},{9,8},{10,11... | collective-permute-start | bytes 1769480 | tf_op jit(solution)/shard_map/ppermute | solution.py:217
  579.0 9.4 %collective-permute-start.26 = (bf16[384,768]{1,0:T(8,128)(2,1)S(1)}, bf16[384,768]{1,0:T(8,128)(2,1)S(1)}, u32[]{:S(2)}, u32[]{:S(2)}) collective-permute-start(bf16[384,768]{1,0:T(8,128)(2,1)S(1)} %copy-done.28), channel_id=1, source_target_pairs={{0,1},{1,0},{2,3},{3,2},{4,5},{5,4},{6,7},{7,6},{8,9},{9,8},{10,11... | collective-permute-start | bytes 1769480 | tf_op jit(solution)/shard_map/ppermute | solution.py:217
  579.1 7.2 %collective-permute-start.23 = (bf16[112,768]{1,0:T(8,128)(2,1)S(1)}, bf16[112,768]{1,0:T(8,128)(2,1)S(1)}, u32[]{:S(2)}, u32[]{:S(2)}) collective-permute-start(bf16[112,768]{1,0:T(8,128)(2,1)S(1)} %add_convert_fusion.5), channel_id=1, source_target_pairs={{0,2},{1,3},{2,0},{3,1},{4,6},{5,7},{6,4},{7,5},{8,10},{9,11},{10,... | collective-permute-start | bytes 516104 | tf_op jit(solution)/shard_map/ppermute | solution.py:217
  580.9 56.9 %collective-permute-start.25 = (bf16[96,3072]{1,0:T(8,128)(2,1)S(1)}, bf16[96,3072]{1,0:T(8,128)(2,1)S(1)}, u32[]{:S(2)}, u32[]{:S(2)}) collective-permute-start(bf16[96,3072]{1,0:T(8,128)(2,1)S(1)} %add_convert_fusion.4), channel_id=1, source_target_pairs={{0,2},{1,3},{2,0},{3,1},{4,6},{5,7},{6,4},{7,5},{8,10},{9,11},{10,... | collective-permute-start | bytes 1769480 | tf_op jit(solution)/shard_map/ppermute | solution.py:217
  588.6 54.0 %collective-permute-start.27 = (bf16[384,768]{1,0:T(8,128)(2,1)S(1)}, bf16[384,768]{1,0:T(8,128)(2,1)S(1)}, u32[]{:S(2)}, u32[]{:S(2)}) collective-permute-start(bf16[384,768]{1,0:T(8,128)(2,1)S(1)} %add_convert_fusion.3), channel_id=1, source_target_pairs={{0,2},{1,3},{2,0},{3,1},{4,6},{5,7},{6,4},{7,5},{8,10},{9,11},{10,... | collective-permute-start | bytes 1769480 | tf_op jit(solution)/shard_map/ppermute | solution.py:217
  (65 other events, 902.7 us)
Sparse Core Ops, SparseCore 0:
  10.2 53.0 all-gather.4
  65.5 82.7 all-gather.6
  150.5 78.1 all-gather.8
  313.1 62.8 reduce-scatter.10
  379.4 94.3 reduce-scatter.6
  477.4 95.1 reduce-scatter.8
  576.5 59.6 reduce-scatter.12
